TPU v7x, 32 devices: a whole 2x2x4 slice. The times are simulated.
32 devices in a mesh: tower: 2 (over x), items: 16 (over z, y, core).
Axes of the slice: x: 2, y: 2, z: 4, core: 2. Of those that a mesh axis runs over, the one named last changes fastest.
Arguments:
- states: bfloat16 [2, 2, 16, 512, 768], P('tower', None, 'items'), may hold values from -6 to 6
- proj_weight: bfloat16 [2, 768, 768], P('tower'), may hold values from -0.21875 to 0.21875
- proj_bias: float32 [2, 768], P('tower'), may hold values from -2 to 2
- cls_row: float32 [768], replicated, may hold values from -6 to 6
- norm1_gain: float32 [768], replicated, may hold values from 0.25 to 1.75
- norm1_shift: float32 [768], replicated, may hold values from -2 to 2
- qkv_weight: bfloat16 [768, 2304], replicated, may hold values from -0.3125 to 0.3125
- qv_bias: float32 [1536], replicated, may hold values from -2 to 2
- out_weight: bfloat16 [768, 768], replicated, may hold values from -3.5 to 3.5
- out_bias: float32 [768], replicated, may hold values from -2 to 2
- norm2_gain: float32 [768], replicated, may hold values from 0.25 to 1.75
- norm2_shift: float32 [768], replicated, may hold values from -2 to 2
- up_weight: bfloat16 [768, 3072], replicated, may hold values from -0.21875 to 0.21875
- up_bias: float32 [3072], replicated, may hold values from -2 to 2
- down_weight: bfloat16 [3072, 768], replicated, may hold values from -0.109375 to 0.109375
- down_bias: float32 [768], replicated, may hold values from -2 to 2
- image_group: int32 [2, 16], P('tower', 'items'), may hold values from 0 to 1
- caption_len: int32 [2, 16], P('tower', 'items'), may hold values from 64 to 512, as said below
- out_grad: bfloat16 [2, 16, 838, 768], P('tower', 'items'), may hold values from -6 to 6
Outputs:
- layer_out: bfloat16 [2, 16, 838, 768], P('tower', 'items')
- state_grad: bfloat16 [2, 2, 16, 512, 768], P('tower', None, 'items')
- proj_weight_grad: float32 [2, 768, 768], P('tower', 'items')
- proj_bias_grad: float32 [2, 768], P('tower', 'items')
- cls_grad: float32 [768], P('items')
- norm1_gain_grad: float32 [768], P('items')
- norm1_shift_grad: float32 [768], P('items')
- qkv_weight_grad: float32 [768, 2304], P('items')
- qv_bias_grad: float32 [1536], P('items')
- out_weight_grad: float32 [768, 768], P('items')
- out_bias_grad: float32 [768], P('items')
- norm2_gain_grad: float32 [768], P('items')
- norm2_shift_grad: float32 [768], P('items')
- up_weight_grad: float32 [768, 3072], P('items')
- up_bias_grad: float32 [3072], P('items')
- down_weight_grad: float32 [3072, 768], P('items')
- down_bias_grad: float32 [768], P('items')
Inputs may be any that keep to these rules, and one draw needn't show every extreme that they name: `image_group`: an image has 197 patch rows where its group is 0 and 325 where it is 1. `caption_len`: some item's caption fills all 512 slots.
All inputs are finite; a program needn't handle non-finite values.
Results may differ from a plain program's by a relative error of at most 0.015.
The roundings to bfloat16 on the way count: a program that leaves them out, or rounds other values in their place, can miss the bound.
Values may be sent and summed in bfloat16 or wider, within the bound.
A program may use at most 256 MiB of HBM per device.

v0:
```python
import jax
import jax.numpy as jnp
from jax import lax
from jax.sharding import PartitionSpec as P

HEADS = 12
HEAD_DIM = 64
PATCH_SMALL = 197
PATCH_BIG = 325


EPSILON = 1e-06
MASKED = -1000000000.0
SCALE = 0.125


def from_partner(block, axis, apart):
    count = lax.axis_size(axis)
    route = []
    for low in range(count):
        high = low | 1 << apart
        if high != low and high < count:
            route += [(low, high), (high, low)]
    return lax.ppermute(block, axis, route)


def layer_norm(inputs, norm_gain, norm_shift):
    row_mean = jnp.mean(inputs, axis=-1, keepdims=True)
    centered = inputs - row_mean
    variance = jnp.mean(centered * centered, axis=-1, keepdims=True)
    return centered * lax.rsqrt(variance + EPSILON) * norm_gain + norm_shift


def exact_gelu(inputs):
    return jax.nn.gelu(inputs, approximate=False)


def masked_scores(queries, key_rows, live_rows):
    raw_scores = (
        jnp.einsum("qhe,khe->hqk", queries, key_rows, preferred_element_type=jnp.float32) * SCALE
    )
    return jnp.where(live_rows[None, None, :], raw_scores, MASKED)


def attend(pieces):
    queries, key_rows, value_rows, live_rows = pieces
    scores = masked_scores(queries, key_rows, live_rows)
    row_max = jnp.max(scores, axis=-1, keepdims=True)
    exponent = jnp.exp(scores - row_max)
    row_total = jnp.sum(exponent, axis=-1, keepdims=True)
    attn_weights = (exponent / row_total).astype(jnp.bfloat16)
    attended = jnp.einsum(
        "hqk,khe->qhe", attn_weights, value_rows, preferred_element_type=jnp.float32
    )
    return (attended.astype(jnp.bfloat16), (row_max + jnp.log(row_total))[..., 0])


def attend_back(pieces):
    queries, key_rows, value_rows, live_rows, log_total, grad_attended = pieces
    scores = masked_scores(queries, key_rows, live_rows)
    attn_weights = jnp.exp(scores - log_total[..., None])
    grad_value = jnp.einsum(
        "hqk,qhe->khe",
        attn_weights.astype(jnp.bfloat16),
        grad_attended,
        preferred_element_type=jnp.float32,
    )
    grad_weights = jnp.einsum(
        "qhe,khe->hqk", grad_attended, value_rows, preferred_element_type=jnp.float32
    )
    inner = jnp.sum(attn_weights * grad_weights, axis=-1, keepdims=True)
    grad_scores = (attn_weights * (grad_weights - inner)).astype(jnp.bfloat16)
    grad_query = (
        jnp.einsum("hqk,khe->qhe", grad_scores, key_rows, preferred_element_type=jnp.float32)
        * SCALE
    )
    grad_key = (
        jnp.einsum("hqk,qhe->khe", grad_scores, queries, preferred_element_type=jnp.float32) * SCALE
    )
    return (grad_query, grad_key, grad_value)


def body(
    states,
    proj_weight,
    proj_bias,
    cls_row,
    norm1_gain,
    norm1_shift,
    qkv_weight,
    qv_bias,
    out_weight,
    out_bias,
    norm2_gain,
    norm2_shift,
    up_weight,
    up_bias,
    down_weight,
    down_bias,
    image_group,
    caption_len,
    out_grad,
):
    on_image_side = lax.axis_index("tower") == 0
    model_width = states.shape[-1]
    slot_count = states.shape[3]
    item_count = states.shape[2]
    own_states = states[0]
    flat_states = own_states.reshape(-1, model_width)
    projected = (
        jnp.dot(flat_states, proj_weight[0], preferred_element_type=jnp.float32) + proj_bias[0]
    )
    projected = projected.astype(jnp.bfloat16).reshape(own_states.shape)
    kept_rows = jnp.where(on_image_side, projected[0], projected[1])
    sent_rows = jnp.where(on_image_side, projected[1], projected[0])
    arrived = from_partner(sent_rows, "tower", 0)
    image_rows = jnp.where(on_image_side, kept_rows, arrived)
    text_rows = jnp.where(on_image_side, arrived, kept_rows)
    cls_block = jnp.broadcast_to(cls_row, (item_count, 1, model_width))
    joined = jnp.concatenate(
        [cls_block, image_rows[:, :PATCH_BIG].astype(jnp.float32), text_rows.astype(jnp.float32)],
        axis=1,
    )
    extent = joined.shape[1]
    position = jnp.arange(extent, dtype=jnp.int32)[None, :]
    patches = PATCH_SMALL + (PATCH_BIG - PATCH_SMALL) * image_group[0][:, None]
    captions = caption_len[0][:, None]
    live_rows = (
        (position == 0)
        | (position >= 1) & (position <= patches)
        | (position > PATCH_BIG) & (position - PATCH_BIG - 1 < captions)
    )
    row_mask = live_rows[..., None].astype(jnp.float32)
    first_normed, norm1_back = jax.vjp(layer_norm, joined, norm1_gain, norm1_shift)
    first_input = first_normed.astype(jnp.bfloat16)
    projected_qkv = jnp.einsum(
        "ard,de->are", first_input, qkv_weight, preferred_element_type=jnp.float32
    )
    head_shape = (item_count, extent, HEADS, HEAD_DIM)
    queries = (
        (projected_qkv[..., :model_width] + qv_bias[:model_width])
        .astype(jnp.bfloat16)
        .reshape(head_shape)
    )
    key_rows = (
        projected_qkv[..., model_width : 2 * model_width].astype(jnp.bfloat16).reshape(head_shape)
    )
    value_rows = (
        (projected_qkv[..., 2 * model_width :] + qv_bias[model_width:])
        .astype(jnp.bfloat16)
        .reshape(head_shape)
    )
    attended, log_total = lax.map(attend, (queries, key_rows, value_rows, live_rows))
    attended = attended.reshape(item_count, extent, model_width)
    branch = (
        jnp.einsum("ard,de->are", attended, out_weight, preferred_element_type=jnp.float32)
        + out_bias
    )
    middle = joined + branch
    second_normed, norm2_back = jax.vjp(layer_norm, middle, norm2_gain, norm2_shift)
    second_input = second_normed.astype(jnp.bfloat16)
    hidden_pre = (
        jnp.einsum("ard,df->arf", second_input, up_weight, preferred_element_type=jnp.float32)
        + up_bias
    )
    activated, gelu_back = jax.vjp(exact_gelu, hidden_pre)
    activated_low = activated.astype(jnp.bfloat16)
    result = (
        middle
        + jnp.einsum("arf,fd->ard", activated_low, down_weight, preferred_element_type=jnp.float32)
        + down_bias
    )
    layer_out = (result * row_mask).astype(jnp.bfloat16)[None]
    grad_result = out_grad[0].astype(jnp.float32) * row_mask
    grad_result_low = grad_result.astype(jnp.bfloat16)
    down_grad = jnp.einsum(
        "arf,ard->fd", activated_low, grad_result_low, preferred_element_type=jnp.float32
    )
    down_bias_part = jnp.sum(grad_result, axis=(0, 1))
    grad_activated = jnp.einsum(
        "ard,fd->arf", grad_result_low, down_weight, preferred_element_type=jnp.float32
    )
    grad_hidden = gelu_back(grad_activated)[0].astype(jnp.bfloat16)
    up_grad = jnp.einsum(
        "ard,arf->df", second_input, grad_hidden, preferred_element_type=jnp.float32
    )
    up_bias_part = jnp.sum(grad_hidden, axis=(0, 1), dtype=jnp.float32)
    grad_second = jnp.einsum(
        "arf,df->ard", grad_hidden, up_weight, preferred_element_type=jnp.float32
    )
    grad_middle_norm, norm2_gain_part, norm2_shift_part = norm2_back(grad_second)
    grad_middle = grad_result + grad_middle_norm
    grad_branch = grad_middle.astype(jnp.bfloat16)
    out_grad_part = jnp.einsum(
        "ard,are->de", attended, grad_branch, preferred_element_type=jnp.float32
    )
    out_bias_part = jnp.sum(grad_branch, axis=(0, 1), dtype=jnp.float32)
    grad_attended = jnp.einsum(
        "are,de->ard", grad_branch, out_weight, preferred_element_type=jnp.float32
    )
    grad_attended = grad_attended.astype(jnp.bfloat16).reshape(head_shape)
    grad_query, grad_key, grad_value = lax.map(
        attend_back, (queries, key_rows, value_rows, live_rows, log_total, grad_attended)
    )
    flat_shape = (item_count, extent, model_width)
    grad_qkv = jnp.concatenate(
        [
            grad_query.reshape(flat_shape),
            grad_key.reshape(flat_shape),
            grad_value.reshape(flat_shape),
        ],
        axis=-1,
    ).astype(jnp.bfloat16)
    qkv_grad = jnp.einsum("ard,are->de", first_input, grad_qkv, preferred_element_type=jnp.float32)
    bias_sums = jnp.sum(grad_qkv, axis=(0, 1), dtype=jnp.float32)
    qv_bias_part = jnp.concatenate([bias_sums[:model_width], bias_sums[2 * model_width :]])
    grad_first = jnp.einsum("are,de->ard", grad_qkv, qkv_weight, preferred_element_type=jnp.float32)
    grad_first_norm, norm1_gain_part, norm1_shift_part = norm1_back(grad_first)
    grad_joined = grad_middle + grad_first_norm
    cls_part = jnp.sum(grad_joined[:, 0], axis=0)
    grad_image = grad_joined[:, 1 : 1 + PATCH_BIG].astype(jnp.bfloat16)
    grad_image = jnp.concatenate(
        [grad_image, jnp.zeros((item_count, slot_count - PATCH_BIG, model_width), jnp.bfloat16)],
        axis=1,
    )
    grad_text = grad_joined[:, 1 + PATCH_BIG :].astype(jnp.bfloat16)
    grad_kept = jnp.where(on_image_side, grad_image, grad_text)
    grad_sent = jnp.where(on_image_side, grad_text, grad_image)
    grad_returned = from_partner(grad_sent, "tower", 0)
    grad_projected = jnp.where(
        on_image_side, jnp.stack([grad_kept, grad_returned]), jnp.stack([grad_returned, grad_kept])
    )
    flat_grad = grad_projected.reshape(-1, model_width)
    proj_grad = jnp.einsum("rd,re->de", flat_states, flat_grad, preferred_element_type=jnp.float32)
    proj_bias_part = jnp.sum(flat_grad, axis=0, dtype=jnp.float32)
    state_grad = jnp.einsum(
        "re,de->rd", flat_grad, proj_weight[0], preferred_element_type=jnp.float32
    )
    state_grad = state_grad.astype(jnp.bfloat16).reshape(states.shape)
    shares = (
        lax.psum_scatter(up_grad, "items", scatter_dimension=0, tiled=True),
        lax.psum_scatter(down_grad, "items", scatter_dimension=0, tiled=True),
        lax.psum_scatter(up_bias_part, "items", scatter_dimension=0, tiled=True),
        lax.psum_scatter(down_bias_part, "items", scatter_dimension=0, tiled=True),
        lax.psum_scatter(norm2_gain_part, "items", scatter_dimension=0, tiled=True),
        lax.psum_scatter(norm2_shift_part, "items", scatter_dimension=0, tiled=True),
        lax.psum_scatter(qkv_grad, "items", scatter_dimension=0, tiled=True),
        lax.psum_scatter(out_grad_part, "items", scatter_dimension=0, tiled=True),
        lax.psum_scatter(proj_grad, "items", scatter_dimension=0, tiled=True),
        lax.psum_scatter(qv_bias_part, "items", scatter_dimension=0, tiled=True),
        lax.psum_scatter(out_bias_part, "items", scatter_dimension=0, tiled=True),
        lax.psum_scatter(norm1_gain_part, "items", scatter_dimension=0, tiled=True),
        lax.psum_scatter(norm1_shift_part, "items", scatter_dimension=0, tiled=True),
        lax.psum_scatter(cls_part, "items", scatter_dimension=0, tiled=True),
        lax.psum_scatter(proj_bias_part, "items", scatter_dimension=0, tiled=True),
    )
    up_share, down_share, up_bias_share, down_bias_share, norm2_gain_share, norm2_shift_share = (
        shares[0:6]
    )
    (
        qkv_share,
        out_share,
        proj_share,
        qv_bias_share,
        out_bias_share,
        norm1_gain_share,
        norm1_shift_share,
        cls_share,
        proj_bias_share,
    ) = shares[6:15]
    summed = (
        lax.psum(cls_share.astype(jnp.bfloat16), "tower").astype(jnp.float32),
        lax.psum(norm1_gain_share.astype(jnp.bfloat16), "tower").astype(jnp.float32),
        lax.psum(norm1_shift_share.astype(jnp.bfloat16), "tower").astype(jnp.float32),
        lax.psum(qkv_share.astype(jnp.bfloat16), "tower").astype(jnp.float32),
        lax.psum(qv_bias_share.astype(jnp.bfloat16), "tower").astype(jnp.float32),
        lax.psum(out_share.astype(jnp.bfloat16), "tower").astype(jnp.float32),
        lax.psum(out_bias_share.astype(jnp.bfloat16), "tower").astype(jnp.float32),
        lax.psum(norm2_gain_share.astype(jnp.bfloat16), "tower").astype(jnp.float32),
        lax.psum(norm2_shift_share.astype(jnp.bfloat16), "tower").astype(jnp.float32),
        lax.psum(up_share.astype(jnp.bfloat16), "tower").astype(jnp.float32),
        lax.psum(up_bias_share.astype(jnp.bfloat16), "tower").astype(jnp.float32),
        lax.psum(down_share.astype(jnp.bfloat16), "tower").astype(jnp.float32),
        lax.psum(down_bias_share.astype(jnp.bfloat16), "tower").astype(jnp.float32),
    )
    return (
        layer_out,
        state_grad,
        proj_share[None],
        proj_bias_share[None],
        summed[0],
        summed[1],
        summed[2],
        summed[3],
        summed[4],
        summed[5],
        summed[6],
        summed[7],
        summed[8],
        summed[9],
        summed[10],
        summed[11],
        summed[12],
    )


def solution(mesh):
    in_specs = (
        P("tower", None, "items", None, None),
        P("tower", None, None),
        P("tower", None),
        P(),
        P(),
        P(),
        P(),
        P(),
        P(),
        P(),
        P(),
        P(),
        P(),
        P(),
        P(),
        P(),
        P("tower", "items"),
        P("tower", "items"),
        P("tower", "items", None, None),
    )
    out_specs = (
        P("tower", "items", None, None),
        P("tower", None, "items", None, None),
        P("tower", "items", None),
        P("tower", "items"),
        P("items"),
        P("items"),
        P("items"),
        P("items", None),
        P("items"),
        P("items", None),
        P("items"),
        P("items"),
        P("items"),
        P("items", None),
        P("items"),
        P("items", None),
        P("items"),
    )
    return jax.shard_map(body, mesh=mesh, in_specs=in_specs, out_specs=out_specs, check_vma=False)
```

profile of v0, /device:TPU:0, one launch (start us, length us, event | category | flops | bytes accessed | tf_op | source)
XLA Modules:
  0.0 718.4 jit_solution(10527886477976966568)
XLA Ops:
  8.1 3.3 add_convert_fusion.1
  11.5 3.0 collective-permute-start
  16.4 15.6 %collective-permute-done = bf16[1,512,768]{2,1,0:T(8,128)(2,1)S(1)} collective-permute-done((bf16[1,512,768]{2,1,0:T(8,128)(2,1)S(1)}, bf16[1,512,768]{2,1,0:T(8,128)(2,1)S(1)}, u32[]{:S(2)}, u32[]{:S(2)}) %collective-permute-start) | collective-permute-done | bytes 786464 | tf_op jit(solution)/shard_map/ppermute | solution.py:24
  33.9 3.6 convolution_bitcast_fusion
  38.7 2.0 fusion.17
  40.7 3.0 copy.61
  43.7 2.5 copy.62
  46.2 2.5 copy.60
  48.7 20.4 %fusion.56 = (f32[12,838]{1,0:T(8,128)S(1)}, f32[12,838,838]{1,2,0:T(8,128)}) fusion(bf16[838,12,64]{0,2,1:T(8,128)(2,1)} %bitcast.115, bf16[838,12,64]{0,2,1:T(8,128)(2,1)} %bitcast.122, pred[838]{0:T(1024)(128)(4,1)S(1)} %get-tuple-element.181), kind=kOutput, calls=%fused_computation.129 | convolution fusion | flops 1103917440 | bytes 36323112 | tf_op jit(solution)/shard_map/while/body/eval_jaxpr/qhe,khe->hqk/dot_general | solution.py:40
  69.1 14.3 %fusion = f32[12,838]{1,0:T(8,128)S(1)} fusion(f32[12,838,838]{1,2,0:T(8,128)} %get-tuple-element.171, f32[12,838]{1,0:T(8,128)S(1)} %get-tuple-element.170), kind=kLoop, calls=%fused_computation.6 | loop fusion | flops 16843800 | bytes 33788160 | tf_op jit(solution)/shard_map/while/body/eval_jaxpr/reduce_sum | solution.py:50
  84.1 16.4 %fusion.22 = bf16[12,64,838]{2,1,0:T(8,128)(2,1)} fusion(bf16[838,12,64]{0,2,1:T(8,128)(2,1)} %bitcast.131, f32[12,838,838]{1,2,0:T(8,128)} %get-tuple-element.171, f32[12,838]{1,0:T(8,128)S(1)} %fusion, f32[12,838]{1,0:T(8,128)S(1)} %get-tuple-element.170), kind=kOutput, calls=%fused_computation.69 | convolution fusion | flops 1104571136 | bytes 36362496 | tf_op jit(solution)/shard_map/while/body/eval_jaxpr/hqk,khe->qhe/dot_general | solution.py:52
  100.6 3.3 fusion.57
  104.8 29.0 %multiply_convert_fusion.1 = (bf16[838,3072]{1,0:T(8,128)(2,1)}, f32[838,3072]{1,0:T(8,128)}, f32[838,3072]{1,0:T(8,128)}) fusion(f32[3072]{0:T(1024)S(1)} %copy-done.38, bf16[768,3072]{1,0:T(8,128)(2,1)S(1)} %bitcast.147, f32[838,768]{1,0:T(8,128)S(1)} %get-tuple-element.173, f32[768]{0:T(1024)S(1)} %copy-done.20, f32[768]{0:T(1024)S(1)} %copy-done.19, ...), kind=kOutput, calls=%fused_computation.15 | convolution fusion | flops 4127304192 | bytes 33061424 | tf_op jit(solution)/shard_map/ard,df->arf/dot_general | solution.py:163
  133.8 12.8 %convert_reduce_fusion = (f32[3072]{0:T(1024)}, bf16[838,3072]{1,0:T(8,128)(2,1)S(1)}) fusion(f32[838,3072]{1,0:T(8,128)} %get-tuple-element.159, bf16[3072,768]{1,0:T(8,128)(2,1)} %param.33, bf16[1,1,838,768]{3,2,1,0:T(8,128)(2,1)S(1)} %copy-done.13, f32[838]{0:T(1024)S(1)} %copy-done.21, f32[838,3072]{1,0:T(8,128)} %get-tuple-element.174, ...), kind=kOutput, calls=%fused_computation.13 | convolution fusion | flops 3999871488 | bytes 31777048 | tf_op jit(solution)/shard_map/ard,fd->arf/dot_general | solution.py:180
  146.6 9.5 %multiply_reduce_fusion.1 = (f32[768]{0:T(1024)}, f32[838]{0:T(1024)S(1)}, f32[768]{0:T(1024)}, f32[838,768]{1,0:T(8,128)S(1)}) fusion(f32[838,768]{1,0:T(8,128)S(1)} %get-tuple-element.173, f32[838]{0:T(1024)S(1)} %fusion.43, f32[838]{0:T(1024)S(1)} %broadcast_multiply_fusion, f32[768]{0:T(1024)S(1)} %copy-done.19, ...), kind=kOutput, calls=%fused_computation.52 | convolution fusion | flops 3959326464 | bytes 15035208 | tf_op jit(solution)/shard_map/arf,df->ard/dot_general | solution.py:188
  159.6 2.8 fusion.58
  162.4 3.9 convolution_convert_fusion.1
  166.4 2.7 copy.64
  169.2 30.3 %multiply_reduce_fusion = (f32[12,838]{1,0:T(8,128)S(1)}, f32[12,838,838]{1,2,0:T(8,128)}) fusion(f32[12,838,838]{1,2,0:T(8,128)} %get-tuple-element.171, f32[12,838]{1,0:T(8,128)} %log_add_fusion, bf16[838,12,64]{0,2,1:T(8,128)(2,1)} %bitcast.124, bf16[838,12,64]{0,2,1:T(8,128)(2,1)} %bitcast.132), kind=kOutput, calls=%fused_computation.1 | convolution fusion | flops 1103917440 | bytes 70070208 | tf_op jit(solution)/shard_map/while/body/eval_jaxpr/qhe,khe->hqk/dot_general | solution.py:68
  199.5 30.1 %multiply_convert_fusion = bf16[12,838,838]{1,2,0:T(8,128)(2,1)} fusion(f32[12,838,838]{1,2,0:T(8,128)} %get-tuple-element.177, f32[12,838,838]{1,2,0:T(8,128)} %get-tuple-element.171, f32[12,838]{1,0:T(8,128)S(1)} %get-tuple-element.176, f32[12,838]{1,0:T(8,128)S(1)} %copy-done.16), kind=kLoop, calls=%fused_computation | loop fusion | flops 33707712 | bytes 84349728 | tf_op jit(solution)/shard_map/while/body/eval_jaxpr/convert_element_type | solution.py:72
  229.6 10.1 %multiply_convert_fusion.2 = bf16[12,64,838]{2,1,0:T(8,128)(2,1)} fusion(bf16[838,12,64]{0,2,1:T(8,128)(2,1)S(1)} %bitcast.116, bf16[12,838,838]{1,2,0:T(8,128)(2,1)} %multiply_convert_fusion), kind=kOutput, calls=%fused_computation.38 | convolution fusion | flops 1079933952 | bytes 19428192 | tf_op jit(solution)/shard_map/while/body/eval_jaxpr/hqk,qhe->khe/dot_general | solution.py:78
  239.7 10.4 %multiply_convert_fusion.3 = bf16[12,64,838]{2,1,0:T(8,128)(2,1)} fusion(bf16[838,12,64]{0,2,1:T(8,128)(2,1)S(1)} %bitcast.123, bf16[12,838,838]{1,2,0:T(8,128)(2,1)} %multiply_convert_fusion), kind=kOutput, calls=%fused_computation.39 | convolution fusion | flops 1079933952 | bytes 19428192 | tf_op jit(solution)/shard_map/while/body/eval_jaxpr/hqk,khe->qhe/dot_general | solution.py:74
  250.1 16.0 %fusion.23 = bf16[12,64,838]{2,1,0:T(8,128)(2,1)} fusion(bf16[838,12,64]{0,2,1:T(8,128)(2,1)} %bitcast.125, f32[12,838,838]{1,2,0:T(8,128)} %get-tuple-element.171, f32[12,838]{1,0:T(8,128)} %log_add_fusion), kind=kOutput, calls=%fused_computation.70 | convolution fusion | flops 1096144256 | bytes 36322272 | tf_op jit(solution)/shard_map/while/body/eval_jaxpr/hqk,qhe->khe/dot_general | solution.py:62
  266.1 10.3 %fusion.20 = f32[768,2304]{1,0:T(8,128)} fusion(bf16[838,768]{0,1:T(8,128)(2,1)} %bitcast.139, bf16[838,768]{0,1:T(8,128)(2,1)} %bitcast.133, bf16[838,768]{0,1:T(8,128)(2,1)} %bitcast.136, f32[768]{0:T(1024)} %param.24, f32[768]{0:T(1024)} %param.23, f32[838]{0:T(1024)} %copy-done.29, f32[838]{0:T(1024)} %copy-done.23, f32[512,768]{1,0:T(8,128)} %bitcast.118, ...), kind=kOutput, calls=%fused_computation.67 | convolution fusion | flops 2981724672 | bytes 13526576 | tf_op jit(solution)/shard_map/ard,are->de/dot_general | solution.py:214
  276.5 10.7 %fusion.47 = f32[768,3072]{1,0:T(8,128)} fusion(bf16[838,3072]{1,0:T(8,128)(2,1)} %copy-done.15, f32[838,768]{1,0:T(8,128)} %copy-done.2, f32[768]{0:T(1024)S(1)} %copy-done.20, f32[768]{0:T(1024)S(1)} %copy-done.19, f32[838]{0:T(1024)S(1)} %fusion.43, f32[838]{0:T(1024)S(1)} %broadcast_multiply_fusion), kind=kOutput, calls=%fused_computation.122 | convolution fusion | flops 3957398016 | bytes 17173040 | tf_op jit(solution)/shard_map/ard,arf->df/dot_general | solution.py:184
  287.9 10.3 %fusion.31 = f32[3072,768]{1,0:T(8,128)} fusion(bf16[838,3072]{1,0:T(8,128)(2,1)} %get-tuple-element.158, bf16[1,1,838,768]{3,2,1,0:T(8,128)(2,1)} %param.37, f32[838]{0:T(1024)S(1)} %copy-done.22), kind=kOutput, calls=%fused_computation.83 | convolution fusion | flops 3956110848 | bytes 15876376 | tf_op jit(solution)/shard_map/arf,ard->fd/dot_general | solution.py:176
  299.0 7.9 %multiply_reduce_fusion.2 = (f32[768]{0:T(1024)}, f32[838]{0:T(1024)S(1)}, f32[768]{0:T(1024)}, f32[838,768]{1,0:T(8,128)S(1)}) fusion(f32[838]{0:T(1024)S(1)} %copy-done.30, f32[838]{0:T(1024)S(1)} %copy-done.24, f32[512,768]{1,0:T(8,128)} %bitcast.119, f32[325,768]{1,0:T(8,128)} %bitcast.128, f32[1,768]{1,0:T(1,128)} %copy-done.32, f32[768]{0:T(1024)} %param.23, ...), kind=kOutput, calls=%fused_computation.54 | convolution fusion | flops 2983653120 | bytes 12568392 | tf_op jit(solution)/shard_map/are,de->ard/dot_general | solution.py:217
  309.1 2.3 fusion.50
  311.9 1.8 collective-permute-start.1
  313.7 17.1 %collective-permute-done.1 = bf16[1,512,768]{2,1,0:T(8,128)(2,1)S(1)} collective-permute-done((bf16[1,512,768]{2,1,0:T(8,128)(2,1)S(1)}, bf16[1,512,768]{2,1,0:T(8,128)(2,1)S(1)}, u32[]{:S(2)}, u32[]{:S(2)}) %collective-permute-start.1) | collective-permute-done | bytes 786464 | tf_op jit(solution)/shard_map/ppermute | solution.py:24
  333.0 2.9 convolution_bitcast_fusion.1
  335.9 3.0 copy.74
  341.8 2.4 fusion.16
  344.1 2.9 convert_reduce_fusion.1
  347.0 9.4 %fusion.27 = bf16[1,1,838,768]{3,2,1,0:T(8,128)(2,1)} fusion(f32[838,768]{1,0:T(8,128)S(1)} %copy-done.3, bf16[838,3072]{1,0:T(8,128)(2,1)} %get-tuple-element.158, bf16[3072,768]{1,0:T(8,128)(2,1)} %param.33, f32[838]{0:T(1024)S(1)} %copy-done.22, f32[768]{0:T(1024)S(1)} %copy-done.41), kind=kOutput, calls=%fused_computation.74 | convolution fusion | flops 3956754432 | bytes 13735192 | tf_op jit(solution)/shard_map/arf,fd->ard/dot_general | solution.py:170
  358.0 10.1 %reduce-scatter.8.cloned.1.call-done = f32[48,2304]{1,0:T(8,128)} async-done(((f32[768,2304]{1,0:T(8,128)}), f32[48,2304]{1,0:T(8,128)}) %reduce-scatter.8.cloned.1.call-update) | async-done | bytes 442384 | tf_op jit(solution)/shard_map/reduce_scatter | solution.py:247
  369.9 113.3 %reduce-scatter.12.cloned.1.call-done = f32[48,3072]{1,0:T(8,128)} async-done(((f32[768,3072]{1,0:T(8,128)}), f32[48,3072]{1,0:T(8,128)}) %reduce-scatter.12.cloned.1.call-update) | async-done | bytes 589840 | tf_op jit(solution)/shard_map/reduce_scatter | solution.py:241
  483.2 1.8 convert_element_type.278
  485.0 113.8 %reduce-scatter.14.cloned.1.call-done = f32[192,768]{1,0:T(8,128)} async-done(((f32[3072,768]{1,0:T(8,128)}), f32[192,768]{1,0:T(8,128)}) %reduce-scatter.14.cloned.1.call-update) | async-done | bytes 589840 | tf_op jit(solution)/shard_map/reduce_scatter | solution.py:242
  598.8 1.8 convert_element_type.283
  601.4 62.0 %all-reduce.11 = (f32[768]{0:T(1024)}, bf16[768]{0:T(1024)(128)(2,1)}, bf16[768]{0:T(1024)(128)(2,1)}, bf16[768]{0:T(1024)(128)(2,1)S(1)}, bf16[1536]{0:T(1024)(...) all-reduce(f32[768]{0:T(1024)} %get-tuple-element.150, ...), channel_id=3, replica_groups=mesh['tower'=2,'items'=16] {'items'}, use_global_device_ids=true, to_apply=%region_13.14.clone | all-reduce | flops 10752 | bytes 66048
  672.0 5.8 all-reduce.12
  689.6 4.3 convolution_convert_fusion
  694.0 1.8 copy.75
  695.8 1.8 copy.69
  697.6 6.8 all-reduce.16.cloned.1.call-done
  707.7 1.8 convert_element_type.279
  709.5 1.8 convert_element_type.284
  (161 shorter events, 44.6 us)
Async XLA Ops:
  7.2 26.7 %copy-start = (bf16[768,2304]{1,0:T(8,128)(2,1)S(1)}, bf16[768,2304]{1,0:T(8,128)(2,1)}, u32[]{:S(2)}) copy-start(bf16[768,2304]{1,0:T(8,128)(2,1)} %param.25) | copy-start | bytes 10616836
  7.2 349.3 %reduce-scatter.10.cloned.1.call-start = ((), (), s32[]{:S(2)}) async-start(), calls=%async_computation.6 | async-start | bytes 2506752 | tf_op jit(solution)/shard_map/reduce_scatter | solution.py:248
  8.1 6.4 copy-start.31
  8.1 8.3 %copy-start.34 = (f32[1536]{0:T(1024)S(1)}, f32[1536]{0:T(1024)}, u32[]{:S(2)}) copy-start(f32[1536]{0:T(1024)} %param.26) | copy-start | bytes 18436
  11.5 20.5 %collective-permute-start = (bf16[1,512,768]{2,1,0:T(8,128)(2,1)S(1)}, bf16[1,512,768]{2,1,0:T(8,128)(2,1)S(1)}, u32[]{:S(2)}, u32[]{:S(2)}) collective-permute-start(bf16[1,512,768]{2,1,0:T(8,128)(2,1)S(1)} %select_bitcast_fusion), channel_id=1, source_target_pairs={{0,16},{16,0},{1,17},{17,1},{2,18},{18,2},{3,19},{19,3},{4,20},{20... | collective-permute-start | bytes 2359304 | tf_op jit(solution)/shard_map/ppermute | solution.py:24
  14.5 86.0 %copy-start.32 = (f32[1,768]{1,0:T(1,128)}, f32[1,768]{1,0:T(1,128)S(1)}, u32[]{:S(2)}) copy-start(f32[1,768]{1,0:T(1,128)S(1)} %concatenate.81) | copy-start | bytes 9220
  32.2 1.7 copy-start.4
  32.3 1.6 copy-start.10
  32.3 1.6 copy-start.35
  32.3 1.6 copy-start.40
  32.7 4.8 copy-start.23
  33.3 4.2 copy-start.29
  84.1 16.4 %copy-start.5 = (f32[1,512,768]{2,1,0:T(8,128)S(1)}, f32[1,512,768]{2,1,0:T(8,128)}, u32[]{:S(2)}) copy-start(f32[1,512,768]{2,1,0:T(8,128)} %copy-done.4) | copy-start | bytes 4718596
  84.1 16.4 %copy-start.11 = (f32[1,325,768]{2,1,0:T(8,128)S(1)}, f32[1,325,768]{2,1,0:T(8,128)}, u32[]{:S(2)}) copy-start(f32[1,325,768]{2,1,0:T(8,128)} %copy-done.10) | copy-start | bytes 2995204
  84.1 16.5 %copy-start.39 = (f32[768]{0:T(1024)S(1)}, f32[768]{0:T(1024)}, u32[]{:S(2)}) copy-start(f32[768]{0:T(1024)} %param.28) | copy-start | bytes 9220
  100.5 3.9 slice-start
  100.6 3.8 slice-start.1
  103.9 52.2 %copy-start.2 = (f32[838,768]{1,0:T(8,128)}, f32[838,768]{1,0:T(8,128)S(1)}, u32[]{:S(2)}) copy-start(f32[838,768]{1,0:T(8,128)S(1)} %get-tuple-element.173) | copy-start | bytes 7723012
  103.9 0.8 copy-start.38
  104.8 29.0 %copy-start.13 = (bf16[1,1,838,768]{3,2,1,0:T(8,128)(2,1)S(1)}, bf16[1,1,838,768]{3,2,1,0:T(8,128)(2,1)}, u32[]{:S(2)}) copy-start(bf16[1,1,838,768]{3,2,1,0:T(8,128)(2,1)} %param.37) | copy-start | bytes 3861508
  104.8 29.0 %copy-start.21 = (f32[838]{0:T(1024)S(1)}, f32[838]{0:T(1024)}, u32[]{:S(2)}) copy-start(f32[838]{0:T(1024)} %get-tuple-element.182) | copy-start | bytes 10060
  146.6 9.5 %copy-start.15 = (bf16[838,3072]{1,0:T(8,128)(2,1)}, bf16[838,3072]{1,0:T(8,128)(2,1)S(1)}, u32[]{:S(2)}) copy-start(bf16[838,3072]{1,0:T(8,128)(2,1)S(1)} %get-tuple-element.180) | copy-start | bytes 15446020
  157.1 1.5 copy-start.7
  157.1 1.5 copy-start.27
  157.1 2.5 copy-start.42
  158.6 1.0 copy-start.18
  166.4 201.8 %reduce-scatter.8.cloned.1.call-start = ((), (), s32[]{:S(2)}) async-start(), calls=%async_computation.5 | async-start | bytes 7520256 | tf_op jit(solution)/shard_map/reduce_scatter | solution.py:247
  169.2 30.3 %copy-start.16 = (f32[12,838]{1,0:T(8,128)S(1)}, f32[12,838]{1,0:T(8,128)}, u32[]{:S(2)}) copy-start(f32[12,838]{1,0:T(8,128)} %log_add_fusion) | copy-start | bytes 120676
  199.5 30.1 %copy-start.1 = (bf16[1,838,768]{1,2,0:T(8,128)(2,1)S(1)}, bf16[1,838,768]{1,2,0:T(8,128)(2,1)}, u32[]{:S(2)}) copy-start(bf16[1,838,768]{1,2,0:T(8,128)(2,1)} %copy.61) | copy-start | bytes 3861508
  229.6 10.1 %copy-start.9 = (bf16[1,838,768]{1,2,0:T(8,128)(2,1)S(1)}, bf16[1,838,768]{1,2,0:T(8,128)(2,1)}, u32[]{:S(2)}) copy-start(bf16[1,838,768]{1,2,0:T(8,128)(2,1)} %copy.62) | copy-start | bytes 3861508
  276.5 206.7 %reduce-scatter.12.cloned.1.call-start = ((), (), s32[]{:S(2)}) async-start(), calls=%async_computation.7 | async-start | bytes 10027008 | tf_op jit(solution)/shard_map/reduce_scatter | solution.py:241
  287.2 311.6 %reduce-scatter.14.cloned.1.call-start = ((), (), s32[]{:S(2)}) async-start(), calls=%async_computation.8 | async-start | bytes 10027008 | tf_op jit(solution)/shard_map/reduce_scatter | solution.py:242
  298.3 8.6 %copy-start.26 = (f32[838]{0:T(1024)S(1)}, f32[838]{0:T(1024)}, u32[]{:S(2)}) copy-start(f32[838]{0:T(1024)} %copy-done.25) | copy-start | bytes 10060
  298.3 395.7 %reduce-scatter.16.cloned.1.call-start = ((), (), s32[]{:S(2)}) async-start(), calls=%async_computation.9 | async-start | bytes 2506752
  298.9 7.9 %copy-start.6 = (f32[1,512,768]{2,1,0:T(8,128)S(1)}, f32[1,512,768]{2,1,0:T(8,128)}, u32[]{:S(2)}) copy-start(f32[1,512,768]{2,1,0:T(8,128)} %copy-done.4) | copy-start | bytes 4718596
  298.9 7.9 %copy-start.12 = (f32[1,325,768]{2,1,0:T(8,128)S(1)}, f32[1,325,768]{2,1,0:T(8,128)}, u32[]{:S(2)}) copy-start(f32[1,325,768]{2,1,0:T(8,128)} %copy-done.10) | copy-start | bytes 2995204
  299.0 7.9 %copy-start.33 = (f32[1,768]{1,0:T(1,128)S(1)}, f32[1,768]{1,0:T(1,128)}, u32[]{:S(2)}) copy-start(f32[1,768]{1,0:T(1,128)} %copy-done.32) | copy-start | bytes 9220
  299.0 7.9 %copy-start.36 = (f32[768]{0:T(1024)S(1)}, f32[768]{0:T(1024)}, u32[]{:S(2)}) copy-start(f32[768]{0:T(1024)} %param.23) | copy-start | bytes 9220
  306.9 1.7 copy-start.8
  306.9 2.2 copy-start.14
  306.9 2.2 copy-start.28
  311.5 21.5 %copy-start.37 = (bf16[1,2,1,512,768]{4,3,2,1,0:T(8,128)(2,1)S(1)}, bf16[1,2,1,512,768]{4,3,2,1,0:T(8,128)(2,1)}, u32[]{:S(2)}) copy-start(bf16[1,2,1,512,768]{4,3,2,1,0:T(8,128)(2,1)} %param.19) | copy-start | bytes 4718596
  311.9 18.8 %collective-permute-start.1 = (bf16[1,512,768]{2,1,0:T(8,128)(2,1)S(1)}, bf16[1,512,768]{2,1,0:T(8,128)(2,1)S(1)}, u32[]{:S(2)}, u32[]{:S(2)}) collective-permute-start(bf16[1,512,768]{2,1,0:T(8,128)(2,1)S(1)} %get-tuple-element.164), channel_id=1, source_target_pairs={{0,16},{16,0},{1,17},{17,1},{2,18},{18,2},{3,19},{19,3},{4,20},{20... | collective-permute-start | bytes 2359304 | tf_op jit(solution)/shard_map/ppermute | solution.py:24
  331.8 1.2 copy-start.17
  335.9 3.3 copy-start.43
  338.9 365.5 %all-reduce.16.cloned.1.call-start = ((), (), s32[]{:S(2)}) async-start(), calls=%async_computation.10 | async-start | bytes 1769472 | tf_op jit(solution)/shard_map/psum | solution.py:275
  341.7 5.3 copy-start.3
  341.7 5.3 copy-start.41
  (6 other events, 4.1 us)
Sparse Core Ops, SparseCore 0:
  166.5 64.4 reduce-scatter.9
  276.6 91.4 reduce-scatter.7
  372.2 110.8 reduce-scatter.11
  487.7 111.0 reduce-scatter.13
  602.4 62.8 reduce-scatter.15
  668.4 35.9 all-reduce.15
where the time goes:
time: 730 us; the launch traced here: 718 us
  waiting for transfers between devices  277 us (38%)
  matrix products  228 us (31%)
  other arithmetic  86.9 us (12%)
  blocking collectives  67.8 us (9%)
  local copies, waits for them, and re-layouts  35.6 us (5%)
  between operations  18.1 us (2%)
    reduce_scatter x1, waiting for transfers between devices, body(): lax.psum_scatter(down_grad, 'items', scatter_dimension=0, tiled=True)  114 us
    reduce_scatter x1, waiting for transfers between devices, body(): lax.psum_scatter(up_grad, 'items', scatter_dimension=0, tiled=True)  113 us
    unnamed x1, blocking collectives  62 us
    ppermute x2, waiting for transfers between devices, from_partner(): return lax.ppermute(block, axis, route)  32.7 us
    dot_general x1, matrix products, attend_back(): jnp.einsum('qhe,khe->hqk', grad_attended, value_rows, preferred_element_t...  30.3 us
    convert_element_type x1, other arithmetic, attend_back(): grad_scores = (attn_weights * (grad_weights - inner)).astype(jnp.bfloat16)  30.1 us
    dot_general x1, matrix products, body(): jnp.einsum('ard,df->arf', second_input, up_weight, preferred_element_type...  29 us
    unnamed x105, local copies, waits for them, and re-layouts  21.5 us
  transfers between devices with their start and end apart: 8, of which 6 were waited for; matrix products, arithmetic and copies ran while one was open for 28% of the time, Pallas kernels for 0%

commit v1 on v0

v1 whole, which is shorter than its diff:
```python
import functools

import jax
import jax.numpy as jnp
from jax import lax
from jax.experimental import pallas as pl
from jax.experimental.pallas import tpu as pltpu
from jax.sharding import PartitionSpec as P

HEADS = 12
HEAD_DIM = 64
PATCH_SMALL = 197
PATCH_BIG = 325
EPSILON = 1e-06
MASKED = -1000000000.0
SCALE = 0.125
ROWS = 896
LANES = 128
TILE_ROWS = 16

F32 = jnp.float32
BF16 = jnp.bfloat16
NN = (((1,), (0,)), ((), ()))
NT = (((1,), (1,)), ((), ()))
TN = (((0,), (0,)), ((), ()))
MESH = pl.DeviceIdType.MESH


def dot(left, right, numbers=NN):
    return lax.dot_general(left, right, numbers, preferred_element_type=F32)


def live_column(group, length, text_rows):
    row = lax.broadcasted_iota(jnp.int32, (ROWS, 1), 0)
    patches = PATCH_SMALL + (PATCH_BIG - PATCH_SMALL) * group
    image = (row >= text_rows) & (row < text_rows + patches)
    return (row < length) | image | (row == text_rows + PATCH_BIG)


def key_lanes(group, length, text_rows):
    lane = lax.broadcasted_iota(jnp.int32, (ROWS, LANES), 1)
    row = lax.broadcasted_iota(jnp.int32, (ROWS, LANES), 0)
    patches = PATCH_SMALL + (PATCH_BIG - PATCH_SMALL) * group
    image = (row >= text_rows) & (row < text_rows + patches)
    live = (row < length) | image | (row == text_rows + PATCH_BIG)
    bias = jnp.where(live, 0.0, MASKED)
    return jnp.where(lane == 0, bias, jnp.where(lane < 4, 1.0, 0.0)).astype(BF16)


def query_lanes(first, column):
    lane = lax.broadcasted_iota(jnp.int32, (ROWS, LANES), 1)
    upper = column.astype(BF16).astype(F32)
    rest = column - upper
    inner = rest.astype(BF16).astype(F32)
    lower = rest - inner
    lanes = jnp.where(lane == 0, first, 0.0)
    lanes = jnp.where(lane == 1, -upper, lanes)
    lanes = jnp.where(lane == 2, -inner, lanes)
    return jnp.where(lane == 3, -lower, lanes).astype(BF16)


def head_part(block, head):
    lane = lax.broadcasted_iota(jnp.int32, block.shape, 1)
    keep = lane < HEAD_DIM if head == 0 else lane >= HEAD_DIM
    return jnp.where(keep, block, jnp.zeros_like(block))


def attention_kernel(text_rows, group_ref, length_ref, qkv_ref, out_ref, total_ref, key_ref):
    width = out_ref.shape[1]
    key_ref[...] = key_lanes(group_ref[0, 0], length_ref[0, 0], text_rows)
    lane = lax.broadcasted_iota(jnp.int32, (ROWS, LANES), 1)
    plain = jnp.where(lane == 0, 1.0, 0.0).astype(BF16)

    @pl.loop(0, width // LANES)
    def pair(index):
        at = pl.multiple_of(index * LANES, LANES)
        queries = qkv_ref[:, pl.ds(at, LANES)]
        keys = qkv_ref[:, pl.ds(pl.multiple_of(width + at, LANES), LANES)]
        values = qkv_ref[:, pl.ds(pl.multiple_of(2 * width + at, LANES), LANES)]
        keys = jnp.concatenate([keys, key_ref[...]], axis=1)
        values = jnp.concatenate([values, key_ref[...]], axis=1)
        scores = []
        for head in range(2):
            own = jnp.concatenate([head_part(queries, head), plain], axis=1)
            scores.append(dot(own, keys, NT))
        outs, totals = [], []
        for head in range(2):
            row_max = jnp.max(scores[head], axis=1, keepdims=True)
            weights = jnp.exp(scores[head] - row_max).astype(BF16)
            mixed = dot(weights, values)
            row_total = mixed[:, LANES + 1 : LANES + 2]
            outs.append(mixed[:, :LANES] / row_total)
            totals.append(row_max + jnp.log(row_total))
        out_ref[:, pl.ds(at, LANES)] = jnp.where(lane < HEAD_DIM, outs[0], outs[1]).astype(BF16)
        total_ref[index] = jnp.where(lane < HEAD_DIM, totals[0], totals[1])


def attention(text_rows, group, length, qkv):
    width = qkv.shape[1] // 3
    pairs = width // LANES
    return pl.pallas_call(
        functools.partial(attention_kernel, text_rows),
        out_shape=(
            jax.ShapeDtypeStruct((ROWS, width), BF16),
            jax.ShapeDtypeStruct((pairs, ROWS, LANES), F32),
        ),
        in_specs=[
            pl.BlockSpec(memory_space=pltpu.SMEM),
            pl.BlockSpec(memory_space=pltpu.SMEM),
            pl.BlockSpec(memory_space=pltpu.VMEM),
        ],
        scratch_shapes=[pltpu.VMEM((ROWS, LANES), BF16)],
        compiler_params=pltpu.CompilerParams(vmem_limit_bytes=52 << 20),
        name="attention_forward",
    )(group, length, qkv)


def attention_back_kernel(
    text_rows, group_ref, length_ref, qkv_ref, total_ref, out_ref, grad_ref, back_ref, key_ref
):
    width = out_ref.shape[1]
    key_ref[...] = key_lanes(group_ref[0, 0], length_ref[0, 0], text_rows)

    @pl.loop(0, width // LANES)
    def pair(index):
        at = pl.multiple_of(index * LANES, LANES)
        key_at = pl.multiple_of(width + at, LANES)
        value_at = pl.multiple_of(2 * width + at, LANES)
        queries = qkv_ref[:, pl.ds(at, LANES)]
        keys = qkv_ref[:, pl.ds(key_at, LANES)]
        values = qkv_ref[:, pl.ds(value_at, LANES)]
        grads = grad_ref[:, pl.ds(at, LANES)]
        product = grads.astype(F32) * out_ref[:, pl.ds(at, LANES)].astype(F32)
        wide_keys = jnp.concatenate([keys, key_ref[...]], axis=1)
        wide_values = jnp.concatenate([values, key_ref[...]], axis=1)
        keys_across = keys.T
        query_grad, key_grad, value_grad = [], None, None
        for head in range(2):
            own_queries = head_part(queries, head)
            own_grads = head_part(grads, head)
            log_total = total_ref[index, :, HEAD_DIM * head : HEAD_DIM * head + 1]
            inner = jnp.sum(head_part(product, head), axis=1, keepdims=True)
            left = jnp.concatenate([own_queries, query_lanes(1.0, log_total)], axis=1)
            right = jnp.concatenate([own_grads, query_lanes(0.0, inner)], axis=1)
            weights = jnp.exp(dot(wide_keys, left, NT))
            score_grad = (weights * dot(wide_values, right, NT)).astype(BF16)
            value_part = dot(weights.astype(BF16), own_grads)
            key_part = dot(score_grad, own_queries)
            value_grad = value_part if value_grad is None else value_grad + value_part
            key_grad = key_part if key_grad is None else key_grad + key_part
            query_grad.append(
                dot(keys_across[HEAD_DIM * head : HEAD_DIM * (head + 1)], score_grad)
            )
        across = jnp.concatenate(query_grad, axis=0).T
        back_ref[:, pl.ds(at, LANES)] = (SCALE * across).astype(BF16)
        back_ref[:, pl.ds(key_at, LANES)] = key_grad.astype(BF16)
        back_ref[:, pl.ds(value_at, LANES)] = value_grad.astype(BF16)


def attention_back(text_rows, group, length, qkv, log_total, attended, grad_attended):
    return pl.pallas_call(
        functools.partial(attention_back_kernel, text_rows),
        out_shape=jax.ShapeDtypeStruct(qkv.shape, BF16),
        in_specs=[pl.BlockSpec(memory_space=pltpu.SMEM)] * 2
        + [pl.BlockSpec(memory_space=pltpu.VMEM)] * 4,
        scratch_shapes=[pltpu.VMEM((ROWS, LANES), BF16)],
        compiler_params=pltpu.CompilerParams(vmem_limit_bytes=56 << 20),
        name="attention_backward",
    )(group, length, qkv, log_total, attended, grad_attended)


def tower_partner():
    return {"tower": 1 - lax.axis_index("tower")}


def item_partner(bit):
    me = lax.axis_index("items")
    low = lax.rem(me // (1 << bit), 2)
    return {"items": me + (1 - 2 * low) * (1 << bit)}, low


def reduce_kernel(bits, units, shared, own_rows, *refs):
    grads, vectors, out_ref, vector_out = refs[:4]
    landed = refs[4 : 4 + bits]
    crossing, crossed, held, vector_here, vector_there = refs[4 + bits : 9 + bits]
    load_sem, send_sem, recv_sem, vector_send, vector_recv = refs[9 + bits :]
    steps = bits + 1

    barrier = pltpu.get_barrier_semaphore()
    partners = [item_partner(bit) for bit in range(bits)]
    for partner, _ in partners:
        pl.semaphore_signal(barrier, inc=1, device_id=partner, device_id_type=MESH)
    pl.semaphore_signal(barrier, inc=1, device_id=tower_partner(), device_id_type=MESH)
    pl.semaphore_wait(barrier, steps)

    lead = (slice(None),)

    def piece(ref, unit, bit, side):
        return ref.at[(unit,) + lead * (bits - 1 - bit) + (side,)]

    def load(unit):
        return pltpu.make_async_copy(
            piece(grads, unit, 0, partners[0][1]), held.at[unit], load_sem.at[unit]
        )

    def send(unit, step):
        if step < bits:
            partner, low = partners[step]
            source = grads if step == 0 else landed[step - 1]
            return pltpu.make_async_remote_copy(
                src_ref=piece(source, unit, step, 1 - low),
                dst_ref=landed[step].at[unit],
                send_sem=send_sem.at[unit, step],
                recv_sem=recv_sem.at[unit, step],
                device_id=partner,
                device_id_type=MESH,
            )
        return pltpu.make_async_remote_copy(
            src_ref=crossing.at[unit],
            dst_ref=crossed.at[unit],
            send_sem=send_sem.at[unit, step],
            recv_sem=recv_sem.at[unit, step],
            device_id=tower_partner(),
            device_id_type=MESH,
        )

    def add(unit, step):
        if step == 0:
            load(unit).wait()
        mine = held.at[unit] if step == 0 else piece(landed[step - 1], unit, step, partners[step][1])
        there = landed[step].at[unit]
        rows = there.shape[-2]
        count = 1 << (bits - 1 - step)

        @pl.loop(0, count)
        def _(number):
            place = tuple(lax.rem(number // (1 << low), 2) for low in reversed(range(bits - 1 - step)))
            total = mine[place].astype(F32) + there[place].astype(F32)
            if step < bits - 1:
                there[place] = total.astype(BF16)
            else:
                crossing[unit] = total.astype(BF16)
                out_ref[unit] = total

    @pl.loop(0, units)
    def _(unit):
        load(unit).start()

    def vector_send_step(step):
        partner = partners[step][0] if step < bits else tower_partner()
        return pltpu.make_async_remote_copy(
            src_ref=vector_here.at[step],
            dst_ref=vector_there.at[step],
            send_sem=vector_send.at[step],
            recv_sem=vector_recv.at[step],
            device_id=partner,
            device_id_type=MESH,
        )

    vector_here[0] = vectors[...]
    vector_send_step(0).start()

    @pl.loop(0, units)
    def _(unit):
        send(unit, 0).start()

    for step in range(steps):
        vector_send_step(step).wait()
        total = vector_here[step] + vector_there[step]
        if step < bits:
            vector_here[step + 1] = total
            vector_send_step(step + 1).start()
        else:
            row = lax.broadcasted_iota(jnp.int32, total.shape, 0)
            vector_out[...] = jnp.where(row == own_rows, vector_here[step], total)

    @pl.loop(0, units + steps - 1)
    def _(wave):
        for step in range(steps):
            unit = wave - step

            @pl.when((unit >= 0) & (unit < (units if step < bits else shared)))
            def _():
                send(unit, step).wait()
                if step < bits:
                    add(unit, step)
                    if step + 1 < bits:
                        send(unit, step + 1).start()
                    else:

                        @pl.when(unit < shared)
                        def _():
                            send(unit, step + 1).start()

                else:
                    out_ref[unit] = crossing[unit].astype(F32) + crossed[unit].astype(F32)


def reduce_all(grads, vectors, bits, shared, own_rows):
    units, rows, width = grads.shape[0], grads.shape[-2], grads.shape[-1]
    landed = [
        pltpu.VMEM((units,) + (2,) * (bits - 1 - step) + (rows, width), BF16)
        for step in range(bits)
    ]
    steps = bits + 1
    return pl.pallas_call(
        functools.partial(reduce_kernel, bits, units, shared, own_rows),
        out_shape=(
            jax.ShapeDtypeStruct((units, rows, width), F32),
            jax.ShapeDtypeStruct(vectors.shape, F32),
        ),
        in_specs=[pl.BlockSpec(memory_space=pl.ANY), pl.BlockSpec(memory_space=pltpu.VMEM)],
        scratch_shapes=landed
        + [
            pltpu.VMEM((units, rows, width), BF16),
            pltpu.VMEM((units, rows, width), BF16),
            pltpu.VMEM((units,) + (2,) * (bits - 1) + (rows, width), BF16),
            pltpu.VMEM((steps,) + vectors.shape, F32),
            pltpu.VMEM((steps,) + vectors.shape, F32),
            pltpu.SemaphoreType.DMA((units,)),
            pltpu.SemaphoreType.DMA((units, steps)),
            pltpu.SemaphoreType.DMA((units, steps)),
            pltpu.SemaphoreType.DMA((steps,)),
            pltpu.SemaphoreType.DMA((steps,)),
        ],
        compiler_params=pltpu.CompilerParams(
            collective_id=1, has_side_effects=True, vmem_limit_bytes=52 << 20
        ),
        name="reduce_gradients",
    )(grads, vectors)


VECTOR_ROWS = 16


def spread_kernel(layout, sums_ref, vectors_ref, *outs):
    me = lax.axis_index("items")
    for (kind, first, count), out_ref in zip(layout, outs):
        if kind == "columns":
            rows, width = sums_ref.shape[1:]
            for part in range(count):
                out_ref[:, part * width : (part + 1) * width] = sums_ref[first + part]
        elif kind == "rows":
            rows = sums_ref.shape[1]
            for part in range(count):
                out_ref[part * rows : (part + 1) * rows, :] = sums_ref[first + part]
        else:
            line = jnp.concatenate(
                [vectors_ref[first + part : first + part + 1, :] for part in range(count)], axis=1
            )
            share = out_ref.shape[1]
            line = jnp.broadcast_to(line, (8, line.shape[1]))
            line = pltpu.roll(line, lax.rem(line.shape[1] - me * share, line.shape[1]), 1)
            out_ref[...] = line[0:1, :share]


def spread(layout, shapes, sums, vectors):
    return pl.pallas_call(
        functools.partial(spread_kernel, layout),
        out_shape=tuple(jax.ShapeDtypeStruct(shape, F32) for shape in shapes),
        in_specs=[pl.BlockSpec(memory_space=pltpu.VMEM)] * 2,
        out_specs=tuple(pl.BlockSpec(memory_space=pltpu.VMEM) for _ in shapes),
        compiler_params=pltpu.CompilerParams(vmem_limit_bytes=32 << 20),
        name="spread_shares",
    )(sums, vectors)


def from_partner(block, axis, apart):
    count = lax.axis_size(axis)
    route = []
    for low in range(count):
        high = low | 1 << apart
        if high != low and high < count:
            route += [(low, high), (high, low)]
    return lax.ppermute(block, axis, route)


def layer_norm(inputs, norm_gain, norm_shift):
    row_mean = jnp.mean(inputs, axis=-1, keepdims=True)
    centered = inputs - row_mean
    variance = jnp.mean(centered * centered, axis=-1, keepdims=True)
    return centered * lax.rsqrt(variance + EPSILON) * norm_gain + norm_shift


def exact_gelu(inputs):
    return jax.nn.gelu(inputs, approximate=False)


def body(
    states,
    proj_weight,
    proj_bias,
    cls_row,
    norm1_gain,
    norm1_shift,
    qkv_weight,
    qv_bias,
    out_weight,
    out_bias,
    norm2_gain,
    norm2_shift,
    up_weight,
    up_bias,
    down_weight,
    down_bias,
    image_group,
    caption_len,
    out_grad,
):
    side = lax.axis_index("tower")
    on_image_side = side == 0
    width = states.shape[-1]
    text_rows = states.shape[3]
    hidden = up_weight.shape[1]
    extent = out_grad.shape[2]
    padding = ROWS - extent
    own_states = states[0].reshape(2 * text_rows, width)
    projected = (dot(own_states, proj_weight[0]) + proj_bias[0]).astype(BF16)
    projected = projected.reshape(2, text_rows, width)
    kept_rows = jnp.where(on_image_side, projected[0], projected[1])
    sent_rows = jnp.where(on_image_side, projected[1], projected[0])
    arrived = from_partner(sent_rows, "tower", 0)
    image_rows = jnp.where(on_image_side, kept_rows, arrived)
    caption_rows = jnp.where(on_image_side, arrived, kept_rows)
    joined = jnp.concatenate(
        [
            caption_rows.astype(F32),
            image_rows[:PATCH_BIG].astype(F32),
            cls_row[None],
            jnp.zeros((padding, width), F32),
        ],
        axis=0,
    )
    group, length = image_group, caption_len
    row_mask = live_column(group[0, 0], length[0, 0], text_rows).astype(F32)
    first_normed, norm1_back = jax.vjp(layer_norm, joined, norm1_gain, norm1_shift)
    first_input = first_normed.astype(BF16)
    scale = jnp.concatenate([jnp.full((width,), SCALE, F32), jnp.ones((2 * width,), F32)])
    bias = jnp.concatenate([qv_bias[:width], jnp.zeros((width,), F32), qv_bias[width:]])
    qkv = ((dot(first_input, qkv_weight) + bias) * scale).astype(BF16)
    attended, log_total = attention(text_rows, group, length, qkv)
    middle = joined + (dot(attended, out_weight) + out_bias)
    second_normed, norm2_back = jax.vjp(layer_norm, middle, norm2_gain, norm2_shift)
    second_input = second_normed.astype(BF16)
    hidden_pre = dot(second_input, up_weight) + up_bias
    activated, gelu_back = jax.vjp(exact_gelu, hidden_pre)
    activated = activated.astype(BF16)
    result = middle + dot(activated, down_weight) + down_bias
    masked = (result * row_mask).astype(BF16)
    layer_out = jnp.concatenate(
        [
            masked[text_rows + PATCH_BIG : extent],
            masked[text_rows : text_rows + PATCH_BIG],
            masked[:text_rows],
        ],
        axis=0,
    )[None, None]
    given = out_grad[0, 0]
    given = jnp.concatenate(
        [
            given[1 + PATCH_BIG :],
            given[1 : 1 + PATCH_BIG],
            given[:1],
            jnp.zeros((padding, width), BF16),
        ],
        axis=0,
    )
    grad_result = given.astype(F32) * row_mask
    grad_low = grad_result.astype(BF16)
    down_grad = dot(activated, grad_low, TN)
    down_bias_part = jnp.sum(grad_result, axis=0)
    grad_hidden = gelu_back(dot(grad_low, down_weight, NT))[0].astype(BF16)
    up_grad = dot(second_input, grad_hidden, TN)
    up_bias_part = jnp.sum(grad_hidden, axis=0, dtype=F32)
    grad_second = dot(grad_hidden, up_weight, NT)
    grad_middle_norm, norm2_gain_part, norm2_shift_part = norm2_back(grad_second)
    grad_middle = grad_result + grad_middle_norm
    grad_branch = grad_middle.astype(BF16)
    out_grad_part = dot(attended, grad_branch, TN)
    out_bias_part = jnp.sum(grad_branch, axis=0, dtype=F32)
    grad_attended = dot(grad_branch, out_weight, NT).astype(BF16)
    grad_qkv = attention_back(text_rows, group, length, qkv, log_total, attended, grad_attended)
    qkv_grad = dot(first_input, grad_qkv, TN)
    bias_sums = jnp.sum(grad_qkv, axis=0, dtype=F32)
    grad_first = dot(grad_qkv, qkv_weight, NT)
    grad_first_norm, norm1_gain_part, norm1_shift_part = norm1_back(grad_first)
    grad_joined = grad_middle + grad_first_norm
    cls_part = grad_joined[text_rows + PATCH_BIG]
    grad_image = grad_joined[text_rows : text_rows + PATCH_BIG].astype(BF16)
    grad_image = jnp.concatenate(
        [grad_image, jnp.zeros((text_rows - PATCH_BIG, width), BF16)], axis=0
    )
    grad_text = grad_joined[:text_rows].astype(BF16)
    grad_kept = jnp.where(on_image_side, grad_image, grad_text)
    grad_sent = jnp.where(on_image_side, grad_text, grad_image)
    grad_returned = from_partner(grad_sent, "tower", 0)
    flat_grad = jnp.where(
        on_image_side,
        jnp.concatenate([grad_kept, grad_returned]),
        jnp.concatenate([grad_returned, grad_kept]),
    )
    proj_grad = dot(own_states, flat_grad, TN)
    proj_bias_part = jnp.sum(flat_grad, axis=0, dtype=F32)
    state_grad = dot(flat_grad, proj_weight[0], NT).astype(BF16).reshape(states.shape)

    items = lax.axis_size("items")
    share = width // items
    bits = items.bit_length() - 1
    parts = hidden // width
    vectors = [
        cls_part, norm1_gain_part, norm1_shift_part, bias_sums[:width], bias_sums[2 * width :],
        out_bias_part, norm2_gain_part, norm2_shift_part, up_bias_part, down_bias_part,
        proj_bias_part,
    ]
    if items != 1 << bits or share % TILE_ROWS:
        return (layer_out, state_grad) + plain_sums(
            proj_grad, qkv_grad, out_grad_part, up_grad, down_grad, vectors
        )
    whole = (2,) * bits
    units = jnp.concatenate(
        [
            up_grad.astype(BF16).reshape(width, parts, width).transpose(1, 0, 2)
            .reshape((parts,) + whole + (share, width)),
            down_grad.astype(BF16).reshape(items, parts, share, width).transpose(1, 0, 2, 3)
            .reshape((parts,) + whole + (share, width)),
            qkv_grad.astype(BF16).reshape(width, 3, width).transpose(1, 0, 2)
            .reshape((3,) + whole + (share, width)),
            out_grad_part.astype(BF16).reshape((1,) + whole + (share, width)),
            proj_grad.astype(BF16).reshape((1,) + whole + (share, width)),
        ],
        axis=0,
    )
    lines = jnp.concatenate(vectors)
    count = lines.shape[0] // width
    lines = jnp.pad(lines, (0, VECTOR_ROWS * width - lines.shape[0])).reshape(VECTOR_ROWS, width)
    shared = 2 * parts + 4
    sums, line_sums = reduce_all(units, lines, bits, shared, count - 1)
    layout = (
        ("rows", shared, 1), ("line", count - 1, 1), ("line", 0, 1), ("line", 1, 1),
        ("line", 2, 1), ("columns", 2 * parts, 3), ("line", 3, 2), ("columns", 2 * parts + 3, 1),
        ("line", 5, 1), ("line", 6, 1), ("line", 7, 1), ("columns", 0, parts),
        ("line", 8, parts), ("rows", parts, parts), ("line", 8 + parts, 1),
    )
    shapes = []
    for kind, _, number in layout:
        if kind == "columns":
            shapes.append((share, number * width))
        elif kind == "rows":
            shapes.append((number * share, width))
        else:
            shapes.append((1, number * share))
    shares = spread(layout, shapes, sums, line_sums)
    shares = [
        piece.reshape(-1) if kind == "line" else piece
        for piece, (kind, _, _) in zip(shares, layout)
    ]
    return (layer_out, state_grad, shares[0][None], shares[1][None]) + tuple(shares[2:])


def plain_sums(proj_grad, qkv_grad, out_grad_part, up_grad, down_grad, vectors):
    def over_items(part):
        return lax.psum_scatter(part, "items", scatter_dimension=0, tiled=True)

    def over_both(part):
        return lax.psum(over_items(part).astype(BF16), "tower").astype(F32)

    cls_part, gain1, shift1, query, value, out_bias, gain2, shift2, up_bias, down_bias, proj = (
        vectors
    )
    return (
        over_items(proj_grad)[None],
        over_items(proj)[None],
        over_both(cls_part),
        over_both(gain1),
        over_both(shift1),
        over_both(qkv_grad),
        over_both(jnp.concatenate([query, value])),
        over_both(out_grad_part),
        over_both(out_bias),
        over_both(gain2),
        over_both(shift2),
        over_both(up_grad),
        over_both(up_bias),
        over_both(down_grad),
        over_both(down_bias),
    )


def solution(mesh):
    in_specs = (
        P("tower", None, "items", None, None),
        P("tower", None, None),
        P("tower", None),
        P(),
        P(),
        P(),
        P(),
        P(),
        P(),
        P(),
        P(),
        P(),
        P(),
        P(),
        P(),
        P(),
        P("tower", "items"),
        P("tower", "items"),
        P("tower", "items", None, None),
    )
    out_specs = (
        P("tower", "items", None, None),
        P("tower", None, "items", None, None),
        P("tower", "items", None),
        P("tower", "items"),
        P("items"),
        P("items"),
        P("items"),
        P("items", None),
        P("items"),
        P("items", None),
        P("items"),
        P("items"),
        P("items"),
        P("items", None),
        P("items"),
        P("items", None),
        P("items"),
    )
    return jax.shard_map(body, mesh=mesh, in_specs=in_specs, out_specs=out_specs, check_vma=False)
```

time: 730 us -> 368 us (0.50); the launches traced: 718 us -> 364 us
  waiting for transfers between devices: 277 us -> 12.9 us
  Pallas kernels: 0 us -> 165 us
  matrix products: 228 us -> 113 us
  blocking collectives: 67.8 us -> 0 us
  other arithmetic: 86.9 us -> 23.5 us
  between operations: 18.1 us -> 3.11 us
  local copies, waits for them, and re-layouts: 35.6 us -> 43.2 us
    reduce_scatter x4 -> x0, waiting for transfers between devices: 237 us -> none  [the longest x1 114 us: body(): lax.psum_scatter(down_grad, 'items', scatter_dimension=0, tiled=True)]
    pallas_call x0 -> x4, Pallas kernels: none -> 165 us  [the longest x1 109 us: reduce_all(): pl.pallas_call(functools.partial(reduce_kernel, bits, units, shared, own_...]
    dot_general x21 -> x15, matrix products: 228 us -> 113 us  [dot(): return lax.dot_general(left, right, numbers, preferred_element_type=F32)]
    unnamed x1 -> x0, blocking collectives: 62 us -> none
    convert_element_type x21 -> x3, other arithmetic: 56.6 us -> 2.88 us  [the longest x1 1.49 us: body(): image_rows[:PATCH_BIG].astype(F32)]
    ppermute x2, waiting for transfers between devices: 32.7 us -> 12.9 us  [from_partner(): return lax.ppermute(block, axis, route)]
    reduce_sum x5 -> x3, other arithmetic: 21.8 us -> 7.13 us  [the longest x1 3.54 us: body(): bias_sums = jnp.sum(grad_qkv, axis=0, dtype=F32)]
    unnamed x105 -> x176, local copies, waits for them, and re-layouts: 21.5 us -> 16.9 us
  transfers between devices with their start and end apart: 8 -> 2, of which waited for: 6 -> 2; matrix products, arithmetic and copies ran while one was open for 28% -> 5% of each run, Pallas kernels for 0% -> 0%
where the time goes in v1:
time: 368 us; the launch traced here: 364 us
  Pallas kernels  165 us (45%)
  matrix products  113 us (31%)
  local copies, waits for them, and re-layouts  43.2 us (12%)
  other arithmetic  23.5 us (6%)
  waiting for transfers between devices  12.9 us (4%)
    dot_general x15, matrix products, dot(): return lax.dot_general(left, right, numbers, preferred_element_type=F32)  113 us
    pallas_call x1, Pallas kernels, reduce_all(): pl.pallas_call(functools.partial(reduce_kernel, bits, units, shared, own_...  109 us
    pallas_call x1, Pallas kernels, attention_back(): pl.pallas_call(functools.partial(attention_back_kernel, text_rows), out_s...  34.4 us
    pallas_call x1, Pallas kernels, attention(): pl.pallas_call(functools.partial(attention_kernel, text_rows), out_shape=...  19.9 us
    unnamed x176, local copies, waits for them, and re-layouts  16.9 us
    ppermute x2, waiting for transfers between devices, from_partner(): return lax.ppermute(block, axis, route)  12.9 us
  transfers between devices with their start and end apart: 2, of which 2 were waited for; matrix products, arithmetic and copies ran while one was open for 5% of the time, Pallas kernels for 0%

profile of v1, /device:TPU:0, one launch (start us, length us, event | category | flops | bytes accessed | tf_op | source)
XLA Modules:
  0.0 364.5 jit_solution(10940774347619949660)
XLA Ops:
  1.6 3.3 add_convert_fusion.1
  4.9 1.1 copy-done.16
  6.0 1.0 broadcast_select_fusion.1
  7.0 2.9 collective-permute-start
  13.4 1.9 slice_bitcast_fusion.1
  15.3 2.2 slice_bitcast_fusion
  17.5 10.3 %collective-permute-done = bf16[512,768]{1,0:T(8,128)(2,1)} collective-permute-done((bf16[512,768]{1,0:T(8,128)(2,1)}, bf16[512,768]{1,0:T(8,128)(2,1)}, u32[]{:S(2)}, u32[]{:S(2)}) %collective-permute-start) | collective-permute-done | bytes 786464 | tf_op jit(solution)/shard_map/ppermute | solution.py:375
  27.8 1.4 select_convert_fusion
  29.2 1.5 fusion.16
  31.8 6.8 %multiply_convert_fusion.1.qkv_ref = bf16[896,2304]{1,0:T(8,128)(2,1)} fusion(bf16[768,2304]{1,0:T(8,128)(2,1)S(1)} %copy-done, f32[2304]{0:T(1024)S(1)} %copy-done.67, f32[2304]{0:T(1024)S(1)} %copy-done.46, f32[768]{0:T(1024)S(1)} %copy-done.64, f32[768]{0:T(1024)S(1)} %copy-done.50, f32[896]{0:T(1024)S(1)} %fusion.21, ...), kind=kOutput, calls=%fused_computation.19 | convolution fusion | flops 3182592000 | bytes 10277376 | tf_op jit(solution)/shard_map/dot_general | solution.py:30
  38.6 19.9 %attention_forward.1 = (bf16[896,768]{1,0:T(8,128)(2,1)S(1)}, f32[6,896,128]{2,1,0:T(8,128)}) custom-call(s32[1,1]{1,0:T(1,128)S(6)} %copy.63.group_ref, s32[1,1]{1,0:T(1,128)} %copy.64.length_ref, bf16[896,2304]{1,0:T(8,128)(2,1)} %multiply_convert_fusion.1.qkv_ref), custom_call_target="tpu_custom_call" | custom-call | tf_op jit(solution)/shard_map/attention_forward/pallas_call | solution.py:101
  58.5 1.5 fusion.31
  60.5 1.2 slice-done.8
  62.2 31.6 %multiply_convert_fusion = (bf16[896,3072]{1,0:T(8,128)(2,1)}, f32[896,3072]{1,0:T(8,128)}, f32[896,3072]{1,0:T(8,128)}) fusion(f32[3072]{0:T(1024)S(1)} %copy-done.60, bf16[768,3072]{1,0:T(8,128)(2,1)S(1)} %bitcast.84, f32[896,768]{1,0:T(8,128)S(1)} %get-tuple-element.113, f32[768]{0:T(1024)S(1)} %copy-done.62, f32[768]{0:T(1024)S(1)} %copy-done.48, ...), kind=kOutput, calls=%fused_computation.4 | convolution fusion | flops 4412964864 | bytes 35021824 | tf_op jit(solution)/shard_map/dot_general | solution.py:30
  93.9 17.4 %convert_reduce_fusion = (f32[3072]{0:T(1024)}, bf16[896,3072]{1,0:T(8,128)(2,1)}) fusion(f32[896,3072]{1,0:T(8,128)} %get-tuple-element.104, bf16[3072,768]{1,0:T(8,128)(2,1)} %param.33, f32[896]{0:T(1024)S(1)} %fusion.19, bf16[896]{0:T(1024)(128)(2,1)} %pad.13.clone, bf16[1,768]{1,0:T(2,128)(2,1)S(1)} %slice_bitcast_fusion.2, ...), kind=kOutput, calls=%fused_computation.2 | convolution fusion | flops 4281529344 | bytes 33560832 | tf_op jit(solution)/shard_map/dot_general | solution.py:30
  111.2 10.5 %multiply_reduce_fusion = (f32[768]{0:T(1024)}, f32[896]{0:T(1024)S(1)}, f32[768]{0:T(1024)}, f32[896,768]{1,0:T(8,128)S(1)}) fusion(f32[896,768]{1,0:T(8,128)} %copy-done.11, f32[896]{0:T(1024)} %copy-done.39, f32[896]{0:T(1024)S(1)} %broadcast_multiply_fusion, f32[768]{0:T(1024)} %param.29, bf16[896,3072]{1,0:T(8,128)(2,1)} %get-tuple-element.118, ...), kind=kOutput, calls=%fused_computation.29 | convolution fusion | flops 4233361152 | bytes 15748608 | tf_op jit(solution)/shard_map/dot_general | solution.py:30
  121.7 7.8 %convolution_convert_fusion.1 = bf16[768,3072]{1,0:T(8,128)(2,1)} fusion(bf16[896,3072]{1,0:T(8,128)(2,1)S(1)} %copy-done.68, f32[896,768]{1,0:T(8,128)S(1)} %copy-done.12, f32[768]{0:T(1024)S(1)} %copy-done.63, f32[768]{0:T(1024)S(1)} %copy-done.49, f32[896]{0:T(1024)S(1)} %copy-done.40, f32[896]{0:T(1024)S(1)} %broadcast_multiply_fusion), kind=kOutput, calls=%fused_computation.21 | convolution fusion | flops 4233658368 | bytes 12989440 | tf_op jit(solution)/shard_map/dot_general | solution.py:30
  129.6 1.0 fusion.28
  130.8 2.9 convert_reduce_fusion.3
  133.7 2.4 convolution_convert_fusion.4.grad_ref
  136.1 34.4 %attention_backward.1 = bf16[896,2304]{1,0:T(8,128)(2,1)} custom-call(s32[1,1]{1,0:T(1,128)S(6)} %copy.63.group_ref, s32[1,1]{1,0:T(1,128)} %copy.64.length_ref, bf16[896,2304]{1,0:T(8,128)(2,1)} %multiply_convert_fusion.1.qkv_ref, f32[6,896,128]{2,1,0:T(8,128)} %get-tuple-element.37.total_ref, bf16[896,768]{1,0:T(8,128)(2,1)} %copy-done.1, ...), custom_call_target="tpu_custom_call" | custom-call | tf_op jit(solution)/shard_map/attention_backward/pallas_call | solution.py:161
  170.5 3.5 convert_reduce_fusion.1
  174.1 6.1 %multiply_reduce_fusion.1 = (f32[768]{0:T(1024)}, f32[896]{0:T(1024)}, f32[768]{0:T(1024)}, f32[896,768]{1,0:T(8,128)}) fusion(f32[896]{0:T(1024)S(1)} %copy-done.42, f32[896]{0:T(1024)S(1)} %broadcast_multiply_fusion.1, f32[896]{0:T(1024)S(1)} %pad.23.clone, f32[1,768]{1,0:T(1,128)S(1)} %broadcast_in_dim.20, f32[325,768]{1,0:T(8,128)S(1)} %copy-done.9, ...), kind=kOutput, calls=%fused_computation.31 | convolution fusion | flops 3178460928 | bytes 13018112 | tf_op jit(solution)/shard_map/dot_general | solution.py:30
  180.2 5.9 %convolution_convert_fusion.2 = bf16[768,2304]{1,0:T(8,128)(2,1)} fusion(bf16[896,2304]{1,0:T(8,128)(2,1)S(1)} %copy-done.7, f32[768]{0:T(1024)S(1)} %copy-done.65, f32[768]{0:T(1024)S(1)} %copy-done.51, f32[896]{0:T(1024)S(1)} %copy-done.42, f32[896]{0:T(1024)S(1)} %broadcast_multiply_fusion.1, f32[1,768]{1,0:T(1,128)S(1)} %broadcast_in_dim.20, ...), kind=kOutput, calls=%fused_computation.22 | convolution fusion | flops 3178168320 | bytes 10258944 | tf_op jit(solution)/shard_map/dot_general | solution.py:30
  186.2 6.5 %convolution_convert_fusion = bf16[3072,768]{1,0:T(8,128)(2,1)S(1)} fusion(bf16[896,3072]{1,0:T(8,128)(2,1)S(1)} %bitcast.101, f32[896]{0:T(1024)S(1)} %fusion.19, bf16[1,768]{1,0:T(2,128)(2,1)S(1)} %slice_bitcast_fusion.2, bf16[325,768]{1,0:T(8,128)(2,1)S(1)} %copy-done.18, bf16[512,768]{1,0:T(8,128)(2,1)S(1)} %copy-done.14, bf16[896]{0:T(1024)(128)(2,1)S(1)} %copy-done.37), kind=kOutput, calls=%fused_computation.20 | convolution fusion | flops 4237099008 | bytes 11516160 | tf_op jit(solution)/shard_map/dot_general | solution.py:30
  192.7 5.6 %multiply_convert_fusion.2 = bf16[896,768]{1,0:T(8,128)(2,1)} fusion(f32[896,768]{1,0:T(8,128)S(1)} %copy-done.13, bf16[896,3072]{1,0:T(8,128)(2,1)S(1)} %bitcast.101, bf16[3072,768]{1,0:T(8,128)(2,1)S(1)} %bitcast.86, f32[896]{0:T(1024)S(1)} %fusion.19, f32[768]{0:T(1024)S(1)} %copy-done.66), kind=kOutput, calls=%fused_computation.39 | convolution fusion | flops 4230610944 | bytes 14359040 | tf_op jit(solution)/shard_map/dot_general | solution.py:30
  198.3 2.8 copy.41
  201.1 1.1 slice-done.4
  202.3 2.5 copy.47
  204.8 5.8 %copy.42 = bf16[768,2304]{0,1:T(8,128)(2,1)} copy(bf16[768,2304]{1,0:T(8,128)(2,1)} %convolution_convert_fusion.2) | data formatting | bytes 7077888 | tf_op jit(solution)/shard_map/convert_element_type | solution.py:526
  210.6 6.1 %copy.43 = bf16[3,768,768]{2,1,0:T(8,128)(2,1)} copy(bf16[3,768,768]{1,2,0:T(8,128)(2,1)} %bitcast.76) | data formatting | bytes 7077888 | tf_op jit(solution)/shard_map/transpose | solution.py:526
  217.4 3.7 %fusion.27 = (f32[896]{0:T(1024)S(1)}, f32[896,768]{1,0:T(8,128)S(1)}) fusion(f32[896]{0:T(1024)S(1)} %multiply_multiply_fusion.5, f32[896]{0:T(1024)S(1)} %broadcast_multiply_fusion.1, f32[896]{0:T(1024)S(1)} %pad.23.clone, f32[1,768]{1,0:T(1,128)S(1)} %broadcast_in_dim.20, f32[325,768]{1,0:T(8,128)} %copy-done.8, f32[512,768]{1,0:T(8,128)} %copy-done.4, ...), kind=kLoop, calls=%fused_computation.105 | loop fusion | flops 6880384 | bytes 8100352 | tf_op jit(solution)/shard_map/transpose(jvp())/reduce_sum | solution.py:380
  221.2 2.6 fusion.26
  225.0 2.7 constant_dynamic-update-slice_fusion.4
  227.7 1.1 slice-done
  229.0 2.7 constant_dynamic-update-slice_fusion.3
  231.7 1.0 copy-done.10
  232.7 2.1 constant_dynamic-update-slice_fusion.2
  236.1 1.5 convolution_convert_fusion.6
  237.6 1.1 constant_dynamic-update-slice_fusion.1
  239.1 1.4 maximum_bitcast_fusion
  240.4 2.6 collective-permute-done.1
  244.5 1.4 reshape.205.refs_1_
  246.0 3.9 %convolution_convert_fusion.5 = bf16[768,768]{0,1:T(8,128)(2,1)S(1)} fusion(bf16[1024,768]{1,0:T(8,128)(2,1)} %bitcast.88, bf16[512,768]{1,0:T(8,128)(2,1)} %copy-done.25, bf16[512,768]{1,0:T(8,128)(2,1)} %copy-done.20, pred[]{:T(512)S(6)} %eq.14), kind=kOutput, calls=%fused_computation.49 | convolution fusion | flops 1215627264 | bytes 4325377 | tf_op jit(solution)/shard_map/dot_general | solution.py:30
  249.9 1.1 constant_dynamic-update-slice_fusion.refs_0_
  251.0 109.3 %reduce_gradients.1 = (f32[13,48,768]{2,1,0:T(8,128)S(1)}, f32[16,768]{1,0:T(8,128)S(1)}) custom-call(bf16[13,2,2,2,2,48,768]{6,5,4,3,2,1,0:T(8,128)(2,1)} %constant_dynamic-update-slice_fusion.refs_0_, f32[16,768]{1,0:T(8,128)S(1)} %copy-done.3), custom_call_target="tpu_custom_call" | custom-call | tf_op jit(solution)/shard_map/reduce_gradients/pallas_call | solution.py:306
  360.3 1.4 spread_shares.1
  361.7 2.6 convolution_convert_fusion.3
  (208 shorter events, 10.5 us)
Async XLA Ops:
  0.7 31.1 %copy-start = (bf16[768,2304]{1,0:T(8,128)(2,1)S(1)}, bf16[768,2304]{1,0:T(8,128)(2,1)}, u32[]{:S(2)}) copy-start(bf16[768,2304]{1,0:T(8,128)(2,1)} %param.25) | copy-start | bytes 10616836
  1.5 9.7 %copy-start.47 = (f32[1536]{0:T(1024)S(1)}, f32[1536]{0:T(1024)}, u32[]{:S(2)}) copy-start(f32[1536]{0:T(1024)} %param.26) | copy-start | bytes 18436
  1.5 10.3 %copy-start.52 = (f32[768]{0:T(1024)S(1)}, f32[768]{0:T(1024)}, u32[]{:S(2)}) copy-start(f32[768]{0:T(1024)} %param.22) | copy-start | bytes 9220
  7.0 20.8 %collective-permute-start = (bf16[512,768]{1,0:T(8,128)(2,1)}, bf16[512,768]{1,0:T(8,128)(2,1)}, u32[]{:S(2)}, u32[]{:S(2)}) collective-permute-start(bf16[512,768]{1,0:T(8,128)(2,1)} %broadcast_select_fusion.1), channel_id=1, source_target_pairs={{0,16},{16,0},{1,17},{17,1},{2,18},{18,2},{3,19},{19,3},{4,20},{20... | collective-permute-start | bytes 2359304 | tf_op jit(solution)/shard_map/ppermute | solution.py:375
  11.9 180.8 %copy-start.30 = (f32[896]{0:T(1024)}, f32[896]{0:T(1024)S(1)}, u32[]{:S(2)}) copy-start(f32[896]{0:T(1024)S(1)} %fusion.19) | copy-start | bytes 10756
  11.9 15.9 %copy-start.17 = (bf16[1024,768]{1,0:T(8,128)(2,1)S(1)}, bf16[1024,768]{1,0:T(8,128)(2,1)}, u32[]{:S(2)}) copy-start(bf16[1024,768]{1,0:T(8,128)(2,1)} %copy-done.16) | copy-start | bytes 4718596
  13.4 172.7 %copy-start.35 = (bf16[1,768]{1,0:T(2,128)(2,1)}, bf16[1,768]{1,0:T(2,128)(2,1)S(1)}, u32[]{:S(2)}) copy-start(bf16[1,768]{1,0:T(2,128)(2,1)S(1)} %slice_bitcast_fusion.2) | copy-start | bytes 4612
  29.2 151.0 %copy-start.4 = (f32[512,768]{1,0:T(8,128)}, f32[512,768]{1,0:T(8,128)S(1)}, u32[]{:S(2)}) copy-start(f32[512,768]{1,0:T(8,128)S(1)} %get-tuple-element.105) | copy-start | bytes 4718596
  30.7 27.8 %copy-start.8 = (f32[325,768]{1,0:T(8,128)}, f32[325,768]{1,0:T(8,128)S(1)}, u32[]{:S(2)}) copy-start(f32[325,768]{1,0:T(8,128)S(1)} %fusion.16) | copy-start | bytes 2995204
  31.7 6.9 %copy-start.28 = (f32[896]{0:T(1024)}, f32[896]{0:T(1024)S(1)}, u32[]{:S(2)}) copy-start(f32[896]{0:T(1024)S(1)} %multiply_reduce_fusion.5) | copy-start | bytes 10756
  31.8 6.9 %copy-start.41 = (f32[896]{0:T(1024)}, f32[896]{0:T(1024)S(1)}, u32[]{:S(2)}) copy-start(f32[896]{0:T(1024)S(1)} %fusion.21) | copy-start | bytes 10756
  38.6 19.9 %copy-start.57 = (bf16[768,768]{1,0:T(8,128)(2,1)S(1)}, bf16[768,768]{1,0:T(8,128)(2,1)}, u32[]{:S(2)}) copy-start(bf16[768,768]{1,0:T(8,128)(2,1)} %param.27) | copy-start | bytes 3538948
  38.6 19.9 %copy-start.61 = (f32[768]{0:T(1024)S(1)}, f32[768]{0:T(1024)}, u32[]{:S(2)}) copy-start(f32[768]{0:T(1024)} %param.28) | copy-start | bytes 9220
  60.0 33.9 %copy-start.11 = (f32[896,768]{1,0:T(8,128)}, f32[896,768]{1,0:T(8,128)S(1)}, u32[]{:S(2)}) copy-start(f32[896,768]{1,0:T(8,128)S(1)} %get-tuple-element.113) | copy-start | bytes 8257540
  62.2 31.6 %copy-start.39 = (f32[896]{0:T(1024)}, f32[896]{0:T(1024)S(1)}, u32[]{:S(2)}) copy-start(f32[896]{0:T(1024)S(1)} %fusion.22) | copy-start | bytes 10756
  111.2 10.5 %copy-start.12 = (f32[896,768]{1,0:T(8,128)S(1)}, f32[896,768]{1,0:T(8,128)}, u32[]{:S(2)}) copy-start(f32[896,768]{1,0:T(8,128)} %copy-done.11) | copy-start | bytes 8257540
  111.2 10.5 %copy-start.40 = (f32[896]{0:T(1024)S(1)}, f32[896]{0:T(1024)}, u32[]{:S(2)}) copy-start(f32[896]{0:T(1024)} %copy-done.39) | copy-start | bytes 10756
  111.2 10.5 %copy-start.49 = (f32[768]{0:T(1024)S(1)}, f32[768]{0:T(1024)}, u32[]{:S(2)}) copy-start(f32[768]{0:T(1024)} %param.29) | copy-start | bytes 9220
  111.2 10.5 %copy-start.63 = (f32[768]{0:T(1024)S(1)}, f32[768]{0:T(1024)}, u32[]{:S(2)}) copy-start(f32[768]{0:T(1024)} %param.30) | copy-start | bytes 9220
  111.2 10.5 %copy-start.68 = (bf16[896,3072]{1,0:T(8,128)(2,1)S(1)}, bf16[896,3072]{1,0:T(8,128)(2,1)}, u32[]{:S(2)}) copy-start(bf16[896,3072]{1,0:T(8,128)(2,1)} %get-tuple-element.118) | copy-start | bytes 16515076
  130.6 5.5 %copy-start.5 = (f32[896,768]{1,0:T(8,128)}, f32[896,768]{1,0:T(8,128)S(1)}, u32[]{:S(2)}) copy-start(f32[896,768]{1,0:T(8,128)S(1)} %get-tuple-element.102) | copy-start | bytes 8257540
  130.7 5.4 %copy-start.32 = (f32[896]{0:T(1024)}, f32[896]{0:T(1024)S(1)}, u32[]{:S(2)}) copy-start(f32[896]{0:T(1024)S(1)} %negate_multiply_fusion.2) | copy-start | bytes 10756
  136.1 38.0 %copy-start.9 = (f32[325,768]{1,0:T(8,128)S(1)}, f32[325,768]{1,0:T(8,128)}, u32[]{:S(2)}) copy-start(f32[325,768]{1,0:T(8,128)} %copy-done.8) | copy-start | bytes 2995204
  170.5 15.6 %slice-start.12 = ((s8[5505024]{0:T(1024)(128)(4,1)}), s8[4194304]{0:T(1024)(128)(4,1)S(1)}, s32[]{:S(2)}) async-start(s8[5505024]{0:T(1024)(128)(4,1)} %bitcast.100), calls=%async_computation.12 | async-start | bytes 8388608
  174.1 6.1 %copy-start.65 = (f32[768]{0:T(1024)S(1)}, f32[768]{0:T(1024)}, u32[]{:S(2)}) copy-start(f32[768]{0:T(1024)} %param.24) | copy-start | bytes 9220
  174.1 12.0 %slice-start.13 = ((s8[5505024]{0:T(1024)(128)(4,1)}), s8[1310720]{0:T(1024)(128)(4,1)S(1)}, s32[]{:S(2)}) async-start(s8[5505024]{0:T(1024)(128)(4,1)} %bitcast.100), calls=%async_computation.13 | async-start | bytes 2621440
  180.2 12.5 %slice-start.10 = ((s8[4718592]{0:T(1024)(128)(4,1)}), s8[524288]{0:T(1024)(128)(4,1)S(1)}, s32[]{:S(2)}) async-start(s8[4718592]{0:T(1024)(128)(4,1)} %bitcast.85), calls=%async_computation.10 | async-start | bytes 1048576
  186.1 6.5 %copy-start.13 = (f32[896,768]{1,0:T(8,128)S(1)}, f32[896,768]{1,0:T(8,128)}, u32[]{:S(2)}) copy-start(f32[896,768]{1,0:T(8,128)} %copy-done.11) | copy-start | bytes 8257540
  186.1 6.5 %slice-start.11 = ((s8[4718592]{0:T(1024)(128)(4,1)}), s8[4194304]{0:T(1024)(128)(4,1)S(1)}, s32[]{:S(2)}) async-start(s8[4718592]{0:T(1024)(128)(4,1)} %bitcast.85), calls=%async_computation.11 | async-start | bytes 8388608
  186.1 6.5 %copy-start.66 = (f32[768]{0:T(1024)S(1)}, f32[768]{0:T(1024)}, u32[]{:S(2)}) copy-start(f32[768]{0:T(1024)} %param.34) | copy-start | bytes 9220
  198.3 3.9 %slice-start.4 = ((s8[4718592]{0:T(1024)(128)(4,1)}), s8[4194304]{0:T(1024)(128)(4,1)S(1)}, s32[]{:S(2)}) async-start(s8[4718592]{0:T(1024)(128)(4,1)} %bitcast.77), calls=%async_computation.4 | async-start | bytes 8388608
  198.3 4.0 %slice-start.5 = ((s8[4718592]{0:T(1024)(128)(4,1)}), s8[524288]{0:T(1024)(128)(4,1)S(1)}, s32[]{:S(2)}) async-start(s8[4718592]{0:T(1024)(128)(4,1)} %bitcast.77), calls=%async_computation.5 | async-start | bytes 1048576
  210.6 6.1 %copy-start.29 = (f32[896]{0:T(1024)S(1)}, f32[896]{0:T(1024)}, u32[]{:S(2)}) copy-start(f32[896]{0:T(1024)} %copy-done.28) | copy-start | bytes 10756
  217.3 3.8 %copy-start.15 = (bf16[512,768]{1,0:T(8,128)(2,1)S(1)}, bf16[512,768]{1,0:T(8,128)(2,1)}, u32[]{:S(2)}) copy-start(bf16[512,768]{1,0:T(8,128)(2,1)} %slice_bitcast_fusion) | copy-start | bytes 2359300
  217.3 3.8 %copy-start.19 = (bf16[325,768]{1,0:T(8,128)(2,1)S(1)}, bf16[325,768]{1,0:T(8,128)(2,1)}, u32[]{:S(2)}) copy-start(bf16[325,768]{1,0:T(8,128)(2,1)} %slice_bitcast_fusion.1) | copy-start | bytes 1497604
  217.3 3.8 %copy-start.31 = (f32[896]{0:T(1024)S(1)}, f32[896]{0:T(1024)}, u32[]{:S(2)}) copy-start(f32[896]{0:T(1024)} %copy-done.30) | copy-start | bytes 10756
  217.3 3.8 %copy-start.33 = (f32[896]{0:T(1024)S(1)}, f32[896]{0:T(1024)}, u32[]{:S(2)}) copy-start(f32[896]{0:T(1024)} %copy-done.32) | copy-start | bytes 10756
  217.3 3.8 %copy-start.36 = (bf16[1,768]{1,0:T(2,128)(2,1)S(1)}, bf16[1,768]{1,0:T(2,128)(2,1)}, u32[]{:S(2)}) copy-start(bf16[1,768]{1,0:T(2,128)(2,1)} %copy-done.35) | copy-start | bytes 4612
  217.4 3.8 %copy-start.38 = (bf16[896]{0:T(1024)(128)(2,1)S(1)}, bf16[896]{0:T(1024)(128)(2,1)}, u32[]{:S(2)}) copy-start(bf16[896]{0:T(1024)(128)(2,1)} %pad.13.clone) | copy-start | bytes 5380
  221.1 3.9 %slice-start.2 = ((s8[4718592]{0:T(1024)(128)(4,1)}), s8[4194304]{0:T(1024)(128)(4,1)S(1)}, s32[]{:S(2)}) async-start(s8[4718592]{0:T(1024)(128)(4,1)} %bitcast.72), calls=%async_computation.2 | async-start | bytes 8388608
  224.2 18.8 %copy-start.20 = (bf16[512,768]{1,0:T(8,128)(2,1)}, bf16[512,768]{1,0:T(8,128)(2,1)S(1)}, u32[]{:S(2)}) copy-start(bf16[512,768]{1,0:T(8,128)(2,1)S(1)} %get-tuple-element.107) | copy-start | bytes 2359300
  224.3 18.8 %collective-permute-start.1 = (bf16[512,768]{1,0:T(8,128)(2,1)S(1)}, bf16[512,768]{1,0:T(8,128)(2,1)S(1)}, u32[]{:S(2)}, u32[]{:S(2)}) collective-permute-start(bf16[512,768]{1,0:T(8,128)(2,1)S(1)} %get-tuple-element.108), channel_id=1, source_target_pairs={{0,16},{16,0},{1,17},{17,1},{2,18},{18,2},{3,19},{19,3},{4,20},{20... | collective-permute-start | bytes 2359304 | tf_op jit(solution)/shard_map/ppermute | solution.py:375
  224.9 3.9 %slice-start = ((s8[4718592]{0:T(1024)(128)(4,1)}), s8[4194304]{0:T(1024)(128)(4,1)S(1)}, s32[]{:S(2)}) async-start(s8[4718592]{0:T(1024)(128)(4,1)} %bitcast.69), calls=%async_computation | async-start | bytes 8388608
  225.0 4.0 %slice-start.1 = ((s8[4718592]{0:T(1024)(128)(4,1)}), s8[524288]{0:T(1024)(128)(4,1)S(1)}, s32[]{:S(2)}) async-start(s8[4718592]{0:T(1024)(128)(4,1)} %bitcast.69), calls=%async_computation.1 | async-start | bytes 1048576
  246.0 5.0 %copy-start.3 = (f32[16,768]{1,0:T(8,128)S(1)}, f32[16,768]{1,0:T(8,128)}, u32[]{:S(2)}) copy-start(f32[16,768]{1,0:T(8,128)} %reshape.205.refs_1_) | copy-start | bytes 147460
  251.0 110.7 %copy-start.21 = (bf16[512,768]{1,0:T(8,128)(2,1)S(1)}, bf16[512,768]{1,0:T(8,128)(2,1)}, u32[]{:S(2)}) copy-start(bf16[512,768]{1,0:T(8,128)(2,1)} %copy-done.20) | copy-start | bytes 2359300
  251.0 110.7 %copy-start.26 = (bf16[512,768]{1,0:T(8,128)(2,1)S(1)}, bf16[512,768]{1,0:T(8,128)(2,1)}, u32[]{:S(2)}) copy-start(bf16[512,768]{1,0:T(8,128)(2,1)} %copy-done.25) | copy-start | bytes 2359300
  251.0 110.7 %copy-start.59 = (bf16[1,768,768]{2,1,0:T(8,128)(2,1)S(1)}, bf16[1,768,768]{2,1,0:T(8,128)(2,1)}, u32[]{:S(2)}) copy-start(bf16[1,768,768]{2,1,0:T(8,128)(2,1)} %param.20) | copy-start | bytes 3538948
  (37 other events, 88.4 us)
